TPU v7x, 32 devices: a whole 2x2x4 slice. The times are simulated.
32 devices in a mesh: wide: 16 (over z, y, core), narrow: 2 (over x).
Axes of the slice: x: 2, y: 2, z: 4, core: 2. Of those that a mesh axis runs over, the one named last changes fastest.
Arguments:
- inputs: bfloat16 [2, 32, 768, 512], P(None, ('wide', 'narrow')), may hold values from -6 to 6
- memory: bfloat16 [2, 32, 96, 512], P(None, ('wide', 'narrow')), may hold values from -6 to 6
- tau_scale: float32 [2, 32], P(None, ('wide', 'narrow')), may hold values from 0.5 to 2
- delta_shift: float32 [2, 32, 96], P(None, ('wide', 'narrow')), may hold values from -32 to 32
- horizon: int32 [2, 32], P(None, ('wide', 'narrow')), may hold values from 96 to 720, as said below
- self_params: bfloat16 [1052672], P(('wide', 'narrow')), may hold values from -2 to 2
- cross_params: bfloat16 [1052672], P(('wide', 'narrow')), may hold values from -2 to 2
- dense_params: bfloat16 [2101248], P(('wide', 'narrow')), may hold values from -2 to 2
- cotangent: bfloat16 [2, 32, 768, 512], P(None, ('wide', 'narrow')), may hold values from -6 to 6
Outputs:
- output: bfloat16 [2, 32, 768, 512], P(None, ('wide', 'narrow'))
- grad_input: float32 [2, 32, 768, 512], P(None, ('wide', 'narrow'))
- grad_memory: float32 [2, 32, 96, 512], P(None, ('wide', 'narrow'))
- grad_self: float32 [1052672], P(('wide', 'narrow'))
- grad_cross: float32 [1052672], P(('wide', 'narrow'))
- grad_dense: float32 [2101248], P(('wide', 'narrow'))
Inputs may be any that keep to these rules, and one draw needn't show every extreme that they name: `horizon`: each entry is one of 96, 192, 336 or 720; the first item of the first micro-batch has 720.
All inputs are finite; a program needn't handle non-finite values.
Results may differ from a plain program's by a relative error of at most 0.025.
The roundings to bfloat16 on the way count: a program that leaves them out, or rounds other values in their place, can miss the bound.
Values may be sent and summed in bfloat16 or wider, within the bound.
No kernel may reach another device: no remote copies, remote signals or barrier semaphores. Data moves between devices by JAX's collectives and lax.ppermute only.
A program may use at most 192 MiB of HBM per device.

v0:
```python
import math

import jax
import jax.numpy as jnp
from jax import lax
from jax.sharding import PartitionSpec as P

D = 512
FF = 2048
HEADS = 8
LABEL = 48


eps_norm = 1e-05
negative = -1e30


def split_attention(flat_params):
    square = D * D
    matrices = [
        flat_params[member * square : (member + 1) * square].reshape(D, D) for member in range(4)
    ]
    offset = 4 * square
    vectors = [flat_params[offset + member * D : offset + (member + 1) * D] for member in range(5)]
    return matrices + vectors


def split_dense(flat_params):
    offset = D * FF
    weight_in = flat_params[:offset].reshape(D, FF)
    weight_out = flat_params[offset : 2 * offset].reshape(FF, D)
    cursor = 2 * offset
    bias_in = flat_params[cursor : cursor + FF]
    cursor = cursor + FF
    vectors = [flat_params[cursor + member * D : cursor + (member + 1) * D] for member in range(3)]
    return [weight_in, weight_out, bias_in] + vectors


def pack_flat(pieces, length):
    flat = jnp.concatenate([piece.reshape(-1) for piece in pieces])
    return jnp.pad(flat, (0, length - flat.shape[0]))


def add_pieces(running, pieces):
    if running is None:
        return pieces
    return [left + right for left, right in zip(running, pieces)]


def project(source, weight):
    return jnp.einsum("isd,df->isf", source, weight, preferred_element_type=jnp.float32)


def project_back(grad_rows, weight):
    return jnp.einsum("isf,df->isd", grad_rows, weight, preferred_element_type=jnp.float32)


def weight_grad(source, grad_rows):
    return jnp.einsum("isd,isf->df", source, grad_rows, preferred_element_type=jnp.float32)


def row_total(values):
    return jnp.sum(values, axis=(0, 1))


def layer_norm(hidden, gain, shift):
    center = hidden - jnp.mean(hidden, -1, keepdims=True)
    spread = jnp.mean(center * center, -1, keepdims=True)
    return center * lax.rsqrt(spread + eps_norm) * gain + shift


def smooth_gate(values):
    return 0.5 * values * (1.0 + lax.erf(values * 0.7071067811865476))


def by_heads(rows):
    item_count, row_count, width = rows.shape
    return jnp.transpose(rows.reshape(item_count, row_count, HEADS, width // HEADS), (2, 0, 1, 3))


def from_heads(stacked):
    head_count, item_count, row_count, head_width = stacked.shape
    return jnp.transpose(stacked, (1, 2, 0, 3)).reshape(
        item_count, row_count, head_count * head_width
    )


def head_scores(head_query, head_key, tau_item, key_shift, causal, row_start):
    raw_scores = jnp.einsum(
        "ise,ime->ism", head_query, head_key, preferred_element_type=jnp.float32
    )
    scores = raw_scores * tau_item[:, None, None]
    if key_shift is not None:
        scores = scores + key_shift[:, None, :]
    scores = scores / math.sqrt(head_query.shape[-1])
    if causal:
        row_place = lax.broadcasted_iota(jnp.int32, scores.shape, 1) + row_start
        col_place = lax.broadcasted_iota(jnp.int32, scores.shape, 2)
        scores = jnp.where(row_place >= col_place, scores, negative)
    return scores


def query_blocks(row_count, causal):
    if causal:
        half = row_count // 2
        return [(0, half, half), (half, row_count, row_count)]
    return [(0, row_count, -1)]


def attend_forward(query_rows, key_rows, value_rows, tau_item, key_shift, causal):
    row_count = query_rows.shape[1]

    def one_head(packed):
        head_query, head_key, head_value = packed
        mixed_parts, log_parts = ([], [])
        for row_start, row_end, key_end in query_blocks(row_count, causal):
            block_key = head_key if key_end < 0 else head_key[:, :key_end]
            block_value = head_value if key_end < 0 else head_value[:, :key_end]
            scores = head_scores(
                head_query[:, row_start:row_end], block_key, tau_item, key_shift, causal, row_start
            )
            row_max = jnp.max(scores, -1, keepdims=True)
            exps = jnp.exp(scores - row_max)
            denominator = jnp.sum(exps, -1, keepdims=True)
            attention_weights = exps / denominator
            mixed_parts.append(
                jnp.einsum(
                    "ism,ime->ise",
                    attention_weights.astype(jnp.bfloat16),
                    block_value,
                    preferred_element_type=jnp.float32,
                )
            )
            log_parts.append((row_max + jnp.log(denominator))[..., 0])
        return (jnp.concatenate(mixed_parts, 1), jnp.concatenate(log_parts, 1))

    mixed_heads, log_totals = lax.map(
        one_head, (by_heads(query_rows), by_heads(key_rows), by_heads(value_rows))
    )
    return (from_heads(mixed_heads).astype(jnp.bfloat16), log_totals)


def attend_backward(
    grad_mixed, query_rows, key_rows, value_rows, log_totals, tau_item, key_shift, causal
):
    row_count = query_rows.shape[1]
    key_count = key_rows.shape[1]

    def one_head(packed):
        head_grad, head_query, head_key, head_value, head_log = packed
        factor = tau_item[:, None, None] / math.sqrt(head_query.shape[-1])
        query_parts = []
        grad_key = jnp.zeros(head_key.shape, jnp.float32)
        grad_value = jnp.zeros(head_value.shape, jnp.float32)
        for row_start, row_end, key_end in query_blocks(row_count, causal):
            block_key = head_key if key_end < 0 else head_key[:, :key_end]
            block_value = head_value if key_end < 0 else head_value[:, :key_end]
            block_query = head_query[:, row_start:row_end]
            block_grad = head_grad[:, row_start:row_end]
            scores = head_scores(block_query, block_key, tau_item, key_shift, causal, row_start)
            attention_weights = jnp.exp(scores - head_log[:, row_start:row_end, None])
            grad_weights = jnp.einsum(
                "ise,ime->ism", block_grad, block_value, preferred_element_type=jnp.float32
            )
            part_value = jnp.einsum(
                "ism,ise->ime",
                attention_weights.astype(jnp.bfloat16),
                block_grad,
                preferred_element_type=jnp.float32,
            )
            row_inner = jnp.sum(attention_weights * grad_weights, -1, keepdims=True)
            grad_raw = (attention_weights * (grad_weights - row_inner) * factor).astype(
                jnp.bfloat16
            )
            query_parts.append(
                jnp.einsum("ism,ime->ise", grad_raw, block_key, preferred_element_type=jnp.float32)
            )
            part_key = jnp.einsum(
                "ism,ise->ime", grad_raw, block_query, preferred_element_type=jnp.float32
            )
            pad_rows = key_count - part_key.shape[1]
            grad_key = grad_key + jnp.pad(part_key, ((0, 0), (0, pad_rows), (0, 0)))
            grad_value = grad_value + jnp.pad(part_value, ((0, 0), (0, pad_rows), (0, 0)))
        return (jnp.concatenate(query_parts, 1), grad_key, grad_value)

    grad_query, grad_key, grad_value = lax.map(
        one_head,
        (
            by_heads(grad_mixed),
            by_heads(query_rows),
            by_heads(key_rows),
            by_heads(value_rows),
            log_totals,
        ),
    )
    return (from_heads(grad_query), from_heads(grad_key), from_heads(grad_value))


def body(
    inputs,
    memory,
    tau_scale,
    delta_shift,
    horizon,
    self_params,
    cross_params,
    dense_params,
    cotangent,
):
    device_count = lax.axis_size(("wide", "narrow"))
    self_length = self_params.shape[0] * device_count
    cross_length = cross_params.shape[0] * device_count
    dense_length = dense_params.shape[0] * device_count
    pieces_self, pieces_cross, pieces_dense = (None, None, None)
    output_rows, input_grads, memory_grads = ([], [], [])
    for micro_step in range(inputs.shape[0]):
        source = inputs[micro_step]
        memory_rows = memory[micro_step]
        tau_item = tau_scale[micro_step]
        key_shift = delta_shift[micro_step]
        horizon_item = horizon[micro_step]
        self_flat, cross_flat = (
            lax.all_gather(self_params, ("wide", "narrow"), axis=0, tiled=True),
            lax.all_gather(cross_params, ("wide", "narrow"), axis=0, tiled=True),
        )
        self_q, self_k, self_v, self_o, self_bq, self_bv, self_bo, gain_one, shift_one = (
            split_attention(self_flat)
        )
        cross_q, cross_k, cross_v, cross_o, cross_bq, cross_bv, cross_bo, gain_two, shift_two = (
            split_attention(cross_flat)
        )
        query_one = (project(source, self_q) + self_bq.astype(jnp.float32)).astype(jnp.bfloat16)
        key_one = project(source, self_k).astype(jnp.bfloat16)
        value_one = (project(source, self_v) + self_bv.astype(jnp.float32)).astype(jnp.bfloat16)
        mixed_one, log_one = attend_forward(query_one, key_one, value_one, tau_item, None, True)
        hidden_one = (
            source.astype(jnp.float32) + project(mixed_one, self_o) + self_bo.astype(jnp.float32)
        )
        first, pull_one = jax.vjp(
            layer_norm, hidden_one, gain_one.astype(jnp.float32), shift_one.astype(jnp.float32)
        )
        first_low = first.astype(jnp.bfloat16)
        query_two = (project(first_low, cross_q) + cross_bq.astype(jnp.float32)).astype(
            jnp.bfloat16
        )
        key_two = project(memory_rows, cross_k).astype(jnp.bfloat16)
        value_two = (project(memory_rows, cross_v) + cross_bv.astype(jnp.float32)).astype(
            jnp.bfloat16
        )
        mixed_two, log_two = attend_forward(
            query_two, key_two, value_two, tau_item, key_shift, False
        )
        hidden_two = first + project(mixed_two, cross_o) + cross_bo.astype(jnp.float32)
        second, pull_two = jax.vjp(
            layer_norm, hidden_two, gain_two.astype(jnp.float32), shift_two.astype(jnp.float32)
        )
        second_low = second.astype(jnp.bfloat16)
        dense_flat = lax.all_gather(dense_params, ("wide", "narrow"), axis=0, tiled=True)
        dense_in, dense_out, bias_in, bias_out, gain_three, shift_three = split_dense(dense_flat)
        pre_gate = project(second_low, dense_in) + bias_in.astype(jnp.float32)
        activated, pull_gate = jax.vjp(smooth_gate, pre_gate)
        activated_low = activated.astype(jnp.bfloat16)
        hidden_three = second + project(activated_low, dense_out) + bias_out.astype(jnp.float32)
        third, pull_three = jax.vjp(
            layer_norm,
            hidden_three,
            gain_three.astype(jnp.float32),
            shift_three.astype(jnp.float32),
        )
        row_place = lax.broadcasted_iota(jnp.int32, third.shape[:2], 1)
        valid_rows = (row_place < LABEL + horizon_item[:, None]).astype(jnp.float32)[..., None]
        output_rows.append((third * valid_rows).astype(jnp.bfloat16))
        dense_flat = lax.all_gather(dense_params, ("wide", "narrow"), axis=0, tiled=True)
        dense_in, dense_out, bias_in, bias_out, gain_three, shift_three = split_dense(dense_flat)
        grad_three, grad_gain_three, grad_shift_three = pull_three(
            cotangent[micro_step].astype(jnp.float32) * valid_rows
        )
        grad_bias_out = row_total(grad_three)
        grad_three_low = grad_three.astype(jnp.bfloat16)
        grad_dense_out = weight_grad(activated_low, grad_three_low)
        (grad_pre_gate,) = pull_gate(project_back(grad_three_low, dense_out))
        grad_bias_in = row_total(grad_pre_gate)
        grad_pre_low = grad_pre_gate.astype(jnp.bfloat16)
        grad_dense_in = weight_grad(second_low, grad_pre_low)
        grad_second = grad_three + project_back(grad_pre_low, dense_in)
        pieces_dense = add_pieces(
            pieces_dense,
            [
                grad_dense_in,
                grad_dense_out,
                grad_bias_in,
                grad_bias_out,
                grad_gain_three,
                grad_shift_three,
            ],
        )
        self_flat, cross_flat = (
            lax.all_gather(self_params, ("wide", "narrow"), axis=0, tiled=True),
            lax.all_gather(cross_params, ("wide", "narrow"), axis=0, tiled=True),
        )
        self_q, self_k, self_v, self_o, self_bq, self_bv, self_bo, gain_one, shift_one = (
            split_attention(self_flat)
        )
        cross_q, cross_k, cross_v, cross_o, cross_bq, cross_bv, cross_bo, gain_two, shift_two = (
            split_attention(cross_flat)
        )
        grad_two, grad_gain_two, grad_shift_two = pull_two(grad_second)
        grad_cross_bo = row_total(grad_two)
        grad_two_low = grad_two.astype(jnp.bfloat16)
        grad_cross_o = weight_grad(mixed_two, grad_two_low)
        grad_mixed_two = project_back(grad_two_low, cross_o).astype(jnp.bfloat16)
        grad_query_two, grad_key_two, grad_value_two = attend_backward(
            grad_mixed_two, query_two, key_two, value_two, log_two, tau_item, key_shift, False
        )
        grad_cross_bq = row_total(grad_query_two)
        grad_cross_bv = row_total(grad_value_two)
        query_two_low = grad_query_two.astype(jnp.bfloat16)
        key_two_low = grad_key_two.astype(jnp.bfloat16)
        value_two_low = grad_value_two.astype(jnp.bfloat16)
        grad_cross_q = weight_grad(first_low, query_two_low)
        grad_cross_k = weight_grad(memory_rows, key_two_low)
        grad_cross_v = weight_grad(memory_rows, value_two_low)
        memory_grads.append(
            project_back(key_two_low, cross_k) + project_back(value_two_low, cross_v)
        )
        grad_first = grad_two + project_back(query_two_low, cross_q)
        pieces_cross = add_pieces(
            pieces_cross,
            [
                grad_cross_q,
                grad_cross_k,
                grad_cross_v,
                grad_cross_o,
                grad_cross_bq,
                grad_cross_bv,
                grad_cross_bo,
                grad_gain_two,
                grad_shift_two,
            ],
        )
        grad_one, grad_gain_one, grad_shift_one = pull_one(grad_first)
        grad_self_bo = row_total(grad_one)
        grad_one_low = grad_one.astype(jnp.bfloat16)
        grad_self_o = weight_grad(mixed_one, grad_one_low)
        grad_mixed_one = project_back(grad_one_low, self_o).astype(jnp.bfloat16)
        grad_query_one, grad_key_one, grad_value_one = attend_backward(
            grad_mixed_one, query_one, key_one, value_one, log_one, tau_item, None, True
        )
        grad_self_bq = row_total(grad_query_one)
        grad_self_bv = row_total(grad_value_one)
        query_one_low = grad_query_one.astype(jnp.bfloat16)
        key_one_low = grad_key_one.astype(jnp.bfloat16)
        value_one_low = grad_value_one.astype(jnp.bfloat16)
        grad_self_q = weight_grad(source, query_one_low)
        grad_self_k = weight_grad(source, key_one_low)
        grad_self_v = weight_grad(source, value_one_low)
        input_grads.append(
            grad_one
            + project_back(query_one_low, self_q)
            + project_back(key_one_low, self_k)
            + project_back(value_one_low, self_v)
        )
        pieces_self = add_pieces(
            pieces_self,
            [
                grad_self_q,
                grad_self_k,
                grad_self_v,
                grad_self_o,
                grad_self_bq,
                grad_self_bv,
                grad_self_bo,
                grad_gain_one,
                grad_shift_one,
            ],
        )
    shard_self, shard_cross, shard_dense = (
        lax.psum_scatter(
            pack_flat(pieces_self, self_length), ("wide", "narrow"), scatter_dimension=0, tiled=True
        ),
        lax.psum_scatter(
            pack_flat(pieces_cross, cross_length),
            ("wide", "narrow"),
            scatter_dimension=0,
            tiled=True,
        ),
        lax.psum_scatter(
            pack_flat(pieces_dense, dense_length),
            ("wide", "narrow"),
            scatter_dimension=0,
            tiled=True,
        ),
    )
    return (
        jnp.stack(output_rows),
        jnp.stack(input_grads),
        jnp.stack(memory_grads),
        shard_self,
        shard_cross,
        shard_dense,
    )


def solution(mesh):
    placed = (
        P(None, ("wide", "narrow"), None, None),
        P(None, ("wide", "narrow"), None, None),
        P(None, ("wide", "narrow")),
        P(None, ("wide", "narrow"), None),
        P(None, ("wide", "narrow")),
        P(("wide", "narrow")),
        P(("wide", "narrow")),
        P(("wide", "narrow")),
        P(None, ("wide", "narrow"), None, None),
    )
    return jax.shard_map(
        body,
        mesh=mesh,
        in_specs=placed,
        out_specs=(
            P(None, ("wide", "narrow"), None, None),
            P(None, ("wide", "narrow"), None, None),
            P(None, ("wide", "narrow"), None, None),
            P(("wide", "narrow")),
            P(("wide", "narrow")),
            P(("wide", "narrow")),
        ),
        check_vma=False,
    )
```

profile of v0, /device:TPU:0, one launch (start us, length us, event | category | flops | bytes accessed | tf_op | source)
XLA Modules:
  0.0 1177.0 jit_solution(7715691930745306727)
XLA Ops:
  27.2 49.1 %all-gather.7.cloned.1.call-done = bf16[32,1,32896]{2,1,0:T(2,128)(2,1)} async-done(((bf16[1,1,32896]{2,1,0:T(2,128)(2,1)}), bf16[32,1,32896]{2,1,0:T(2,128)(2,1)}) %all-gather.7.cloned.1.call-update) | async-done | bytes 2105360 | tf_op jit(solution)/shard_map/all_gather | solution.py:223
  76.3 14.3 %reduce.158 = bf16[32,32896]{1,0:T(8,128)(2,1)} reduce(bf16[32,1,32896]{2,1,0:T(2,128)(2,1)} %all-gather.7.cloned.1.call-done, bf16[]{:T(256)} %constant.336), dimensions={1}, to_apply=%all-gather.reduce_sub_computation | reduce | bytes 4210690 | tf_op jit(solution)/shard_map/all_gather | solution.py:223
  90.6 5.5 reshape.2137
  96.1 2.9 fusion.298
  99.8 40.7 %all-gather.9.cloned.1.call-done = bf16[32,1,32896]{2,1,0:T(2,128)(2,1)} async-done(((bf16[1,1,32896]{2,1,0:T(2,128)(2,1)}), bf16[32,1,32896]{2,1,0:T(2,128)(2,1)}) %all-gather.9.cloned.1.call-update) | async-done | bytes 2105360 | tf_op jit(solution)/shard_map/all_gather | solution.py:224
  140.5 14.1 %reduce.159 = bf16[32,32896]{1,0:T(8,128)(2,1)} reduce(bf16[32,1,32896]{2,1,0:T(2,128)(2,1)} %all-gather.9.cloned.1.call-done, bf16[]{:T(256)} %constant.336), dimensions={1}, to_apply=%all-gather.1.reduce_sub_computation | reduce | bytes 4210690 | tf_op jit(solution)/shard_map/all_gather | solution.py:224
  154.5 5.5 reshape.2139
  160.1 3.0 fusion.297
  183.3 2.5 copy.104
  187.7 42.0 %while.110 = (s32[]{:T(128)}, bf16[8,1,768,64]{2,3,1,0:T(8,128)(2,1)S(1)}, f32[8,1,768]{2,1,0:T(1,128)S(1)}, bf16[8,1,768,64]{3,2,1,0:T(8,128)(2,1)}, bf16[8,1,7...) while((s32[]{:T(128)}, ...), condition=%wide.region_5.6_spmd, body=%wide.region_0.5_spmd.sunk | while | flops 117866880 | bytes 7021681 | solution.py:137
  229.7 2.6 slice.383
  237.9 2.5 copy.105
  242.6 22.3 %while.111 = (s32[]{:T(128)}, bf16[8,1,768,64]{2,3,1,0:T(8,128)(2,1)S(1)}, f32[8,1,768]{2,1,0:T(1,128)S(1)}, bf16[8,1,768,64]{3,2,1,0:T(8,128)(2,1)}, bf16[8,1,9...) while((s32[]{:T(128)}, ...), condition=%wide.region_11.12_spmd, body=%wide.region_8.11_spmd.sunk | while | flops 19537152 | bytes 1364065 | solution.py:137
  264.9 2.5 slice.398
  267.4 3.0 fusion.307
  270.4 2.5 copy.112
  276.4 42.7 %while.112 = (s32[]{:T(128)}, bf16[8,1,768,64]{2,3,1,0:T(8,128)(2,1)S(1)}, f32[8,1,768]{2,1,0:T(1,128)S(1)}, bf16[8,1,768,64]{3,2,1,0:T(8,128)(2,1)}, bf16[8,1,7...) while((s32[]{:T(128)}, ...), condition=%wide.region_21.22_spmd, body=%wide.region_16.21_spmd.sunk | while | flops 117866880 | bytes 7021681 | solution.py:137
  329.7 22.9 %while.113 = (s32[]{:T(128)}, bf16[8,1,768,64]{2,3,1,0:T(8,128)(2,1)S(1)}, f32[8,1,768]{2,1,0:T(1,128)S(1)}, bf16[8,1,768,64]{3,2,1,0:T(8,128)(2,1)}, bf16[8,1,9...) while((s32[]{:T(128)}, ...), condition=%wide.region_27.28_spmd, body=%wide.region_24.27_spmd.sunk | while | flops 19537152 | bytes 1364065 | solution.py:137
  356.3 26.3 %reduce.160 = bf16[32,65664]{1,0:T(8,128)(2,1)} reduce(bf16[32,1,65664]{2,1,0:T(2,128)(2,1)} %all-gather.11.cloned.1.call-done, bf16[]{:T(256)} %constant.336), dimensions={1}, to_apply=%all-gather.2.reduce_sub_computation | reduce | bytes 8404994 | tf_op jit(solution)/shard_map/all_gather | solution.py:258
  382.6 8.6 reshape.2141
  391.1 3.8 fusion.296
  396.4 4.2 slice.403
  400.6 2.7 slice.406
  403.3 4.2 fusion.274
  407.5 4.3 multiply_convert_fusion.7
  419.4 3.2 fusion.289
  422.6 5.2 fusion.313
  428.7 3.9 fusion.232
  433.4 5.2 fusion.312
  438.6 3.9 fusion.189
  444.3 3.3 multiply_reduce_fusion.7
  453.5 55.6 %while.114 = (s32[]{:T(128)}, f32[8,1,768,64]{2,3,1,0:T(8,128)S(1)}, bf16[8,1,96,64]{2,3,1,0:T(8,128)(2,1)S(1)}, f32[8,1,96,64]{2,3,1,0:T(8,128)S(1)}, bf16[8,1,...) while((s32[]{:T(128)}, f32[8,1,768,64]{2,3,1,0:T(8,128)S(1)}, ...), condition=%wide.region_38.39_spmd, body=%wide.region_36.38_spmd.sunk | while | flops 47996160 | bytes 3355653 | solution.py:186
  513.9 61.4 %while.116 = (s32[]{:T(128)}, f32[8,1,768,64]{2,3,1,0:T(8,128)S(1)}, bf16[8,1,96,64]{2,3,1,0:T(8,128)(2,1)S(1)}, f32[8,1,96,64]{2,3,1,0:T(8,128)}, bf16[8,1,768,...) while((s32[]{:T(128)}, f32[8,1,768,64]{2,3,1,0:T(8,128)S(1)}, ...), condition=%wide.region_51.52_spmd, body=%wide.region_49.51_spmd.sunk | while | flops 47996160 | bytes 3355781 | solution.py:186
  596.9 92.5 %while.115 = (s32[]{:T(128)}, f32[8,1,768,64]{2,3,1,0:T(8,128)S(1)}, bf16[8,1,768,64]{2,3,1,0:T(8,128)(2,1)}, f32[8,1,768,64]{2,3,1,0:T(8,128)}, bf16[8,1,768,64...) while((s32[]{:T(128)}, f32[8,1,768,64]{2,3,1,0:T(8,128)S(1)}, ...), condition=%wide.region_44.45_spmd, body=%wide.region_41.44_spmd.sunk | while | flops 288571008 | bytes 17134224 | solution.py:186
  692.7 2.5 copy.138
  697.7 99.1 %while.117 = (s32[]{:T(128)}, f32[8,1,768,64]{2,3,1,0:T(8,128)}, bf16[8,1,768,64]{2,3,1,0:T(8,128)(2,1)}, f32[8,1,768,64]{2,3,1,0:T(8,128)}, bf16[8,1,768,64]{3,...) while((s32[]{:T(128)}, f32[8,1,768,64]{2,3,1,0:T(8,128)}, ...), condition=%wide.region_57.58_spmd, body=%wide.region_54.57_spmd.sunk | while | flops 288571008 | bytes 17134732 | solution.py:186
  803.9 2.5 bitcast_convert_fusion.1
  808.4 3.2 copy.176
  815.2 2.4 constant_dynamic-update-slice_fusion.5
  822.4 2.5 copy.173
  826.8 2.6 copy.172
  840.5 2.5 copy.144
  843.0 2.9 copy.169
  848.5 2.5 copy.143
  851.1 2.5 copy.168
  866.1 9.0 pad.38
  893.0 2.4 copy.148
  900.5 264.4 %all-reduce.13.cloned.1.call-done = (f32[1052672]{0:T(1024)}, f32[1052672]{0:T(1024)}, f32[2101248]{0:T(1024)}) async-done(((f32[1052672]{0:T(1024)}, f32[1052672]{0:T(1024)}, f32[2101248]{0:T(1024)}), (f32[1052672]{0:T(1024)}, f32[1052672]{0:T(1024)}, f32[2101248]{0:T(1024)})) %all-reduce.13.cloned.1.call-update) | async-done | bytes 16826384
  (1281 shorter events, 622.8 us)
Async XLA Ops:
  7.2 69.2 %all-gather.7.cloned.1.call-start = ((), (), s32[]{:S(2)}) async-start(), calls=%async_computation | async-start | bytes 4342272 | tf_op jit(solution)/shard_map/all_gather | solution.py:223
  8.8 131.6 %all-gather.9.cloned.1.call-start = ((), (), s32[]{:S(2)}) async-start(), calls=%async_computation.1 | async-start | bytes 4342272 | tf_op jit(solution)/shard_map/all_gather | solution.py:224
  10.5 345.7 %all-gather.11.cloned.1.call-start = ((), (), s32[]{:S(2)}) async-start(), calls=%async_computation.2 | async-start | bytes 8667648 | tf_op jit(solution)/shard_map/all_gather | solution.py:258
  12.3 1152.5 %all-reduce.13.cloned.1.call-start = ((), (), s32[]{:S(2)}) async-start(), calls=%async_computation.3 | async-start | bytes 33652736
  23.1 67.5 %copy-start.32 = (bf16[1,1,768,512]{2,3,1,0:T(8,128)(2,1)}, bf16[1,1,768,512]{2,3,1,0:T(8,128)(2,1)S(1)}, u32[]{:S(2)}) copy-start(bf16[1,1,768,512]{2,3,1,0:T(8,128)(2,1)S(1)} %copy.166) | copy-start | bytes 2359300
  99.8 252.9 %copy-start.109 = (f32[512]{0:T(512)}, f32[512]{0:T(512)S(1)}, u32[]{:S(2)}) copy-start(f32[512]{0:T(512)S(1)} %get-tuple-element.1005) | copy-start | bytes 6148
  99.8 252.9 %copy-start.145 = (f32[512]{0:T(512)}, f32[512]{0:T(512)S(1)}, u32[]{:S(2)}) copy-start(f32[512]{0:T(512)S(1)} %get-tuple-element.1006) | copy-start | bytes 6148
  163.8 72.4 %copy-start.157 = (f32[512]{0:T(512)}, f32[512]{0:T(512)S(1)}, u32[]{:S(2)}) copy-start(f32[512]{0:T(512)S(1)} %get-tuple-element.1000) | copy-start | bytes 6148
  163.8 103.6 %copy-start.155 = (f32[512]{0:T(512)}, f32[512]{0:T(512)S(1)}, u32[]{:S(2)}) copy-start(f32[512]{0:T(512)S(1)} %get-tuple-element.998) | copy-start | bytes 6148
  163.8 250.5 %copy-start.142 = (f32[512]{0:T(512)}, f32[512]{0:T(512)S(1)}, u32[]{:S(2)}) copy-start(f32[512]{0:T(512)S(1)} %get-tuple-element.996) | copy-start | bytes 6148
  163.8 250.5 %copy-start.148 = (f32[512]{0:T(512)}, f32[512]{0:T(512)S(1)}, u32[]{:S(2)}) copy-start(f32[512]{0:T(512)S(1)} %get-tuple-element.997) | copy-start | bytes 6148
  229.7 4.5 copy-start.4
  229.7 4.5 copy-start.93
  234.3 33.1 %copy-start.24 = (f32[768,512]{0,1:T(8,128)}, f32[768,512]{0,1:T(8,128)S(1)}, u32[]{:S(2)}) copy-start(f32[768,512]{0,1:T(8,128)S(1)} %get-tuple-element.1052) | copy-start | bytes 4718596
  234.5 32.9 %copy-start.103 = (f32[768]{0:T(1024)}, f32[768]{0:T(1024)S(1)}, u32[]{:S(2)}) copy-start(f32[768]{0:T(1024)S(1)} %fusion.255) | copy-start | bytes 9220
  237.9 4.7 copy-start.9
  264.9 5.6 copy-start.6
  264.9 5.6 copy-start.83
  264.9 5.6 copy-start.94
  322.2 30.5 %copy-start.21 = (f32[768,512]{0,1:T(8,128)}, f32[768,512]{0,1:T(8,128)S(1)}, u32[]{:S(2)}) copy-start(f32[768,512]{0,1:T(8,128)S(1)} %get-tuple-element.1056) | copy-start | bytes 4718596
  323.6 29.1 %copy-start.98 = (f32[768]{0:T(1024)}, f32[768]{0:T(1024)S(1)}, u32[]{:S(2)}) copy-start(f32[768]{0:T(1024)S(1)} %fusion.258) | copy-start | bytes 9220
  329.7 23.0 %copy-start.156 = (f32[512]{0:T(512)S(1)}, f32[512]{0:T(512)}, u32[]{:S(2)}) copy-start(f32[512]{0:T(512)} %copy-done.155) | copy-start | bytes 6148
  354.9 92.8 %copy-start.101 = (f32[768]{0:T(1024)}, f32[768]{0:T(1024)S(1)}, u32[]{:S(2)}) copy-start(f32[768]{0:T(1024)S(1)} %broadcast_multiply_fusion.1) | copy-start | bytes 9220
  356.2 91.5 %copy-start.119 = (f32[768]{0:T(1024)}, f32[768]{0:T(1024)S(1)}, u32[]{:S(2)}) copy-start(f32[768]{0:T(1024)S(1)} %fusion.259) | copy-start | bytes 9220
  403.3 4.2 copy-start.51
  403.3 4.2 copy-start.75
  407.5 4.3 copy-start.49
  407.5 4.3 copy-start.76
  422.6 19.9 %copy-start.46 = (f32[768,512]{0,1:T(8,128)}, f32[768,512]{0,1:T(8,128)S(1)}, u32[]{:S(2)}) copy-start(f32[768,512]{0,1:T(8,128)S(1)} %get-tuple-element.954) | copy-start | bytes 4718596
  422.6 19.9 %copy-start.121 = (f32[768]{0:T(1024)}, f32[768]{0:T(1024)S(1)}, u32[]{:S(2)}) copy-start(f32[768]{0:T(1024)S(1)} %negate_multiply_fusion.2) | copy-start | bytes 9220
  427.8 14.6 %copy-start.163 = (bf16[768,2048]{1,0:T(8,128)(2,1)}, bf16[768,2048]{1,0:T(8,128)(2,1)S(1)}, u32[]{:S(2)}) copy-start(bf16[768,2048]{1,0:T(8,128)(2,1)S(1)} %get-tuple-element.1069) | copy-start | bytes 9437188
  433.4 5.2 copy-start.143
  433.4 5.2 copy-start.149
  449.1 134.4 %copy-start.12 = (f32[768,512]{0,1:T(8,128)}, f32[768,512]{0,1:T(8,128)S(1)}, u32[]{:S(2)}) copy-start(f32[768,512]{0,1:T(8,128)S(1)} %get-tuple-element.1039) | copy-start | bytes 4718596
  575.4 8.2 copy-start.73
  576.2 4.9 copy-start.17
  588.0 4.3 copy-start.14
  799.1 7.3 copy-start.167
  800.8 5.5 copy-start.165
  806.4 5.2 copy-start.164
  808.4 3.9 copy-start.162
  860.0 4.2 copy-start.124
  860.0 4.2 copy-start.125
  860.0 5.4 copy-start.126
  860.1 5.4 copy-start.127
  860.1 15.0 %slice-start = ((s8[4206592]{0:T(1024)(128)(4,1)}), s8[12288]{0:T(1024)(128)(4,1)S(1)}, s32[]{:S(2)}) async-start(s8[4206592]{0:T(1024)(128)(4,1)} %bitcast.1015), calls=%async_computation.4 | async-start | bytes 24576
  866.1 9.0 slice-start.1
  866.1 9.0 copy-start.64
  (126 other events, 243.6 us)
Sparse Core Ops, SparseCore 0:
  11.4 64.8 all-gather.6
  79.7 60.6 all-gather.8
  144.0 76.1 all-gather.10
  883.9 280.8 all-reduce.12
where the time goes:
time: 1190 us; the launch traced here: 1180 us
  matrix products  432 us (36%)
  waiting for transfers between devices  354 us (30%)
  local copies, waits for them, and re-layouts  248 us (21%)
  other arithmetic  120 us (10%)
  between operations  18.9 us (2%)
    unnamed x5, waiting for transfers between devices  264 us
    dot_general x96, matrix products, head_scores(): jnp.einsum('ise,ime->ism', head_query, head_key, preferred_element_type=j...  136 us
    unnamed x382, local copies, waits for them, and re-layouts  84.5 us
    squeeze x64, local copies, waits for them, and re-layouts, attend_forward(): lax.map(one_head, (by_heads(query_rows), by_heads(key_rows), by_heads(val...  50.9 us
    all_gather x1, waiting for transfers between devices, body(): lax.all_gather(self_params, ('wide', 'narrow'), axis=0, tiled=True)  49.1 us
    dot_general x48, matrix products, one_head(): jnp.einsum('ism,ise->ime', attention_weights.astype(jnp.bfloat16), block_...  43.1 us
    dot_general x48, matrix products, one_head(): jnp.einsum('ise,ime->ism', block_grad, block_value, preferred_element_typ...  42.1 us
    dot_general x48, matrix products, one_head(): jnp.einsum('ism,ime->ise', attention_weights.astype(jnp.bfloat16), block_...  41.7 us
  transfers between devices with their start and end apart: 4, of which 3 were waited for; matrix products, arithmetic and copies ran while one was open for 22% of the time, Pallas kernels for 0%

commit v1 on v0

v1 whole, which is shorter than its diff:
```python
import functools
import math

import jax
import jax.numpy as jnp
from jax import lax
from jax.experimental import pallas as pl
from jax.experimental.pallas import tpu as pltpu
from jax.sharding import PartitionSpec as P

D = 512
FF = 2048
HEADS = 8
HW = D // HEADS
LABEL = 48
LANES = 128
CH = 256
EPS = 1e-05
NEG = -1e30
LOG2E = 1.4426950408889634
f32, bf16 = jnp.float32, jnp.bfloat16
VMEM_LIMIT = 60 * 2**20


def dot(a, b):
    return jnp.dot(a, b, preferred_element_type=f32)


def dot_nt(a, b):
    return lax.dot_general(a, b, (((1,), (1,)), ((), ())), preferred_element_type=f32)


def norm_stats(h):
    center = h - jnp.mean(h, -1, keepdims=True)
    rstd = lax.rsqrt(jnp.mean(center * center, -1, keepdims=True) + EPS)
    return center * rstd, rstd


def norm_back(dz, n, rstd, gain):
    dn = dz * gain
    return rstd * (dn - jnp.mean(dn, -1, keepdims=True) - n * jnp.mean(dn * n, -1, keepdims=True))


def col_sum(v):
    return jnp.sum(v, 0, keepdims=True)


def load_flat(order, near_ref, far_ref, flat, real):
    half = near_ref.shape[0]

    @pl.loop(0, half)
    def _(k):
        flat[pl.ds(order[k] * real, real), :] = near_ref[k, :real, :].astype(f32)
        flat[pl.ds(order[half + k] * real, real), :] = far_ref[k, :real, :].astype(f32)


def store_flat(order, near_ref, far_ref, flat, real):
    half, rows = near_ref.shape[:2]

    @pl.loop(0, half)
    def _(k):
        near_ref[k] = flat[pl.ds(order[k] * real, rows), :].astype(bf16)
        far_ref[k] = flat[pl.ds(order[half + k] * real, rows), :].astype(bf16)


def take_matrix(flat, start, height, width, put):
    per = width // LANES
    for j in range(per):
        put(j, flat[pl.ds(start + j, height, stride=per), :])


def take_vector(flat, start, width):
    return jnp.concatenate([flat[start + j : start + j + 1, :] for j in range(width // LANES)], 1)


def put_matrix(flat, start, height, width, get):
    per = width // LANES
    for j in range(per):
        flat[pl.ds(start + j, height, stride=per), :] = get(j)


def put_vector(flat, start, row):
    for j in range(row.shape[1] // LANES):
        flat[start + j : start + j + 1, :] = row[:, j * LANES : (j + 1) * LANES]


MAT_ROWS = D * D // LANES


def load_attention(order, near_ref, far_ref, flat, real, w_ref, vec_ref):
    load_flat(order, near_ref, far_ref, flat, real)
    for m in range(4):

        def put(j, block, m=m):
            w_ref[:, m * D + j * LANES : m * D + (j + 1) * LANES] = block.astype(bf16)

        take_matrix(flat, m * MAT_ROWS, D, D, put)
    for i in range(5):
        vec_ref[i : i + 1, :] = take_vector(flat, 4 * MAT_ROWS + i * (D // LANES), D)


def store_attention(order, near_ref, far_ref, flat, real, acc, vec_ref):
    for m in range(4):
        put_matrix(
            flat, m * MAT_ROWS, D, D, lambda j, m=m: acc[:, m * D + j * LANES : m * D + (j + 1) * LANES]
        )
    flat[4 * MAT_ROWS :, :] = jnp.zeros((flat.shape[0] - 4 * MAT_ROWS, LANES), f32)
    for i in range(5):
        put_vector(flat, 4 * MAT_ROWS + i * (D // LANES), vec_ref[i : i + 1, :])
    store_flat(order, near_ref, far_ref, flat, real)


def head_rhs(rows_t, head):
    block = rows_t[head * HW : (head + 1) * HW, :]
    zero = jnp.zeros_like(block)
    return jnp.concatenate([block, zero] if head % 2 == 0 else [zero, block], 0)


def pair_masks(shape, dtype):
    lane = lax.broadcasted_iota(jnp.int32, shape, 1)
    low = lane < HW
    return low.astype(f32).astype(dtype), jnp.logical_not(low).astype(f32).astype(dtype)


def causal_cut(scores, fill):
    keys = scores.shape[0]
    tail = scores[keys - CH :, :]
    key_at = lax.broadcasted_iota(jnp.int32, tail.shape, 0)
    query_at = lax.broadcasted_iota(jnp.int32, tail.shape, 1)
    tail = jnp.where(key_at <= query_at, tail, fill)
    if keys == CH:
        return tail
    return jnp.concatenate([scores[: keys - CH, :], tail], 0)


def self_forward_kernel(
    nch, order, tau, x_ref, pn_ref, pf_ref, q_o, qt_o, k_o, kt_o, v_o, at_o, h_o, lse_o, w_o, vec_o,
    flat, w, vec, ksc, vtsc, at, qt, *, real, chunks,
):
    item, chunk = pl.program_id(0), pl.program_id(1)

    @pl.when((item == 0) & (chunk == 0))
    def _():
        load_attention(order, pn_ref, pf_ref, flat, real, w, vec)
        w_o[...] = w[...]
        vec_o[...] = vec[...]

    @pl.when(chunk < nch[item])
    def _():
        scale = tau[item] * (LOG2E / math.sqrt(HW))
        x = x_ref[0]
        qkv = dot(x, w[:, : 3 * D])
        q = (qkv[:, :D] + vec[0:1, :]).astype(bf16)
        k = qkv[:, D : 2 * D].astype(bf16)
        v = (qkv[:, 2 * D :] + vec[1:2, :]).astype(bf16)
        q_o[0] = q
        k_o[0] = k
        v_o[0] = v
        qt[...] = q.T
        qt_o[0] = qt[...]
        kt_o[0] = k.T
        ksc[pl.ds(pl.multiple_of(chunk * CH, CH), CH), :] = k
        vtsc[:, pl.ds(pl.multiple_of(chunk * CH, CH), CH)] = v.T
        for at_chunk in range(chunks):

            @pl.when(chunk == at_chunk)
            def _(keys=(at_chunk + 1) * CH):
                for head in range(HEADS):
                    pair = head // 2
                    raw = dot(ksc[:keys, pair * LANES : (pair + 1) * LANES], head_rhs(qt, head))
                    s = causal_cut(raw * scale, NEG)
                    top = jnp.max(s, 0, keepdims=True)
                    e = jnp.exp2(s - top)
                    total = jnp.sum(e, 0, keepdims=True)
                    mixed = dot(vtsc[head * HW : (head + 1) * HW, :keys], e.astype(bf16))
                    at[head * HW : (head + 1) * HW, :] = (mixed * (1.0 / total)).astype(bf16)
                    lse_o[0, head : head + 1, :] = top + jnp.log2(total)

        at_o[0] = at[...]
        a = at[...].T
        h_o[0] = x.astype(f32) + dot(a, w[:, 3 * D :]) + vec[2:3, :]


def self_forward(nch, order, tau, x, params, real):
    items, steps, _ = x.shape
    chunks = steps // CH
    half, rows, _ = params[0].shape

    def row_block(i, c, nch_ref, _):
        return (i, jnp.minimum(c, nch_ref[i] - 1), 0)

    def col_block(i, c, nch_ref, _):
        return (i, 0, jnp.minimum(c, nch_ref[i] - 1))

    rowspec = pl.BlockSpec((1, CH, D), row_block)
    colspec = pl.BlockSpec((1, D, CH), col_block)
    whole2 = lambda i, c, *_: (0, 0)
    shards = pl.BlockSpec((half, rows, LANES), lambda i, c, *_: (0, 0, 0), pipeline_mode=pl.Buffered(1))
    shape = jax.ShapeDtypeStruct
    return pl.pallas_call(
        functools.partial(self_forward_kernel, real=real, chunks=chunks),
        grid_spec=pltpu.PrefetchScalarGridSpec(
            num_scalar_prefetch=2,
            grid=(items, chunks),
            in_specs=[
                pl.BlockSpec(memory_space=pltpu.SMEM),
                rowspec,
                shards, shards,
            ],
            out_specs=[
                rowspec, colspec, rowspec, colspec, rowspec, colspec, rowspec,
                pl.BlockSpec((1, HEADS, CH), col_block),
                pl.BlockSpec((D, 4 * D), whole2, pipeline_mode=pl.Buffered(1)),
                pl.BlockSpec((8, D), whole2, pipeline_mode=pl.Buffered(1)),
            ],
            scratch_shapes=[
                pltpu.VMEM((2 * half * real + 16, LANES), f32),
                pltpu.VMEM((D, 4 * D), bf16),
                pltpu.VMEM((8, D), f32),
                pltpu.VMEM((steps, D), bf16),
                pltpu.VMEM((D, steps), bf16),
                pltpu.VMEM((D, CH), bf16),
                pltpu.VMEM((D, CH), bf16),
            ],
        ),
        out_shape=[
            shape((items, steps, D), bf16), shape((items, D, steps), bf16),
            shape((items, steps, D), bf16), shape((items, D, steps), bf16),
            shape((items, steps, D), bf16), shape((items, D, steps), bf16),
            shape((items, steps, D), f32), shape((items, HEADS, steps), f32),
            shape((D, 4 * D), bf16), shape((8, D), f32),
        ],
        compiler_params=pltpu.CompilerParams(vmem_limit_bytes=VMEM_LIMIT),
        cost_estimate=pl.CostEstimate(flops=int(8e9), bytes_accessed=int(2e7), transcendentals=0),
        name="self_forward",
    )(nch, order, tau, x, *params)


def cross_forward_kernel(
    nch, order, tau, h_ref, m_ref, shift_ref, pn_ref, pf_ref, vec1_ref, q_o, qt_o, k_o, kt_o, v_o, at_o, h_o, lse_o, w_o, vec_o,
    flat, w, vec, vtsc, at, qt, *, real, mem,
):
    item, chunk = pl.program_id(0), pl.program_id(1)

    @pl.when((item == 0) & (chunk == 0))
    def _():
        load_attention(order, pn_ref, pf_ref, flat, real, w, vec)
        w_o[...] = w[...]
        vec_o[...] = vec[...]

    @pl.when(chunk == 0)
    def _():
        kv = dot(m_ref[0], w[:, D : 3 * D])
        k = kv[:, :D].astype(bf16)
        v = (kv[:, D:] + vec[1:2, :]).astype(bf16)
        k_o[0] = k
        kt_o[0] = k.T
        v_o[0] = v
        vtsc[...] = v.T

    @pl.when(chunk < nch[item])
    def _():
        scale = tau[item] * (LOG2E / math.sqrt(HW))
        shift = shift_ref[0] * (LOG2E / math.sqrt(HW))
        n1, _ = norm_stats(h_ref[0])
        x1 = n1 * vec1_ref[3:4, :] + vec1_ref[4:5, :]
        q = (dot(x1.astype(bf16), w[:, :D]) + vec[0:1, :]).astype(bf16)
        q_o[0] = q
        qt[...] = q.T
        qt_o[0] = qt[...]
        for head in range(HEADS):
            pair = head // 2
            raw = dot(k_o[0, :, pair * LANES : (pair + 1) * LANES], head_rhs(qt, head))
            s = raw * scale + shift
            top = jnp.max(s, 0, keepdims=True)
            e = jnp.exp2(s - top)
            total = jnp.sum(e, 0, keepdims=True)
            mixed = dot(vtsc[head * HW : (head + 1) * HW, :], e.astype(bf16))
            at[head * HW : (head + 1) * HW, :] = (mixed * (1.0 / total)).astype(bf16)
            lse_o[0, head : head + 1, :] = top + jnp.log2(total)
        at_o[0] = at[...]
        a = at[...].T
        h_o[0] = x1 + dot(a, w[:, 3 * D :]) + vec[2:3, :]


def cross_forward(nch, order, tau, h1, memory, shift, params, vec1, real):
    items, steps, _ = h1.shape
    mem = memory.shape[1]
    chunks = steps // CH
    half, rows, _ = params[0].shape

    def row_block(i, c, nch_ref, _):
        return (i, jnp.minimum(c, nch_ref[i] - 1), 0)

    def col_block(i, c, nch_ref, _):
        return (i, 0, jnp.minimum(c, nch_ref[i] - 1))

    per_item = lambda i, c, *_: (i, 0, 0)
    rowspec = pl.BlockSpec((1, CH, D), row_block)
    colspec = pl.BlockSpec((1, D, CH), col_block)
    memspec = pl.BlockSpec((1, mem, D), per_item)
    whole2 = lambda i, c, *_: (0, 0)
    shards = pl.BlockSpec((half, rows, LANES), lambda i, c, *_: (0, 0, 0), pipeline_mode=pl.Buffered(1))
    shape = jax.ShapeDtypeStruct
    return pl.pallas_call(
        functools.partial(cross_forward_kernel, real=real, mem=mem),
        grid_spec=pltpu.PrefetchScalarGridSpec(
            num_scalar_prefetch=2,
            grid=(items, chunks),
            in_specs=[
                pl.BlockSpec(memory_space=pltpu.SMEM),
                rowspec,
                memspec,
                pl.BlockSpec((1, mem, 1), per_item),
                shards, shards,
                pl.BlockSpec((8, D), whole2, pipeline_mode=pl.Buffered(1)),
            ],
            out_specs=[
                rowspec, colspec, memspec,
                pl.BlockSpec((1, D, mem), per_item),
                memspec, colspec, rowspec,
                pl.BlockSpec((1, HEADS, CH), col_block),
                pl.BlockSpec((D, 4 * D), whole2, pipeline_mode=pl.Buffered(1)),
                pl.BlockSpec((8, D), whole2, pipeline_mode=pl.Buffered(1)),
            ],
            scratch_shapes=[
                pltpu.VMEM((2 * half * real + 16, LANES), f32),
                pltpu.VMEM((D, 4 * D), bf16),
                pltpu.VMEM((8, D), f32),
                pltpu.VMEM((D, mem), bf16),
                pltpu.VMEM((D, CH), bf16),
                pltpu.VMEM((D, CH), bf16),
            ],
        ),
        out_shape=[
            shape((items, steps, D), bf16), shape((items, D, steps), bf16),
            shape((items, mem, D), bf16), shape((items, D, mem), bf16),
            shape((items, mem, D), bf16), shape((items, D, steps), bf16),
            shape((items, steps, D), f32), shape((items, HEADS, steps), f32),
            shape((D, 4 * D), bf16), shape((8, D), f32),
        ],
        compiler_params=pltpu.CompilerParams(vmem_limit_bytes=VMEM_LIMIT),
        cost_estimate=pl.CostEstimate(flops=int(4e9), bytes_accessed=int(2e7), transcendentals=0),
        name="cross_forward",
    )(nch, order, tau, h1, memory, shift, *params, vec1)


def dense_kernel(
    nch, order, horizon, h_ref, ct_ref, pn_ref, pf_ref, vec2_ref, y_o, dh2_o, gn_o, gf_o, small_o,
    flat, w_in, w_out, bias_in, vec, acc_in, acc_out, acc_bias, acc_vec, f_sc, gp_sc, *, real,
):
    item, chunk = pl.program_id(0), pl.program_id(1)
    first = (item == 0) & (chunk == 0)
    last = (item == pl.num_programs(0) - 1) & (chunk == pl.num_programs(1) - 1)
    mat = D * FF // LANES

    @pl.when(first)
    def _():
        load_flat(order, pn_ref, pf_ref, flat, real)

        def put_in(j, block):
            w_in[:, j * LANES : (j + 1) * LANES] = block.astype(bf16)

        def put_out(j, block):
            w_out[:, j * LANES : (j + 1) * LANES] = block.astype(bf16)

        take_matrix(flat, 0, D, FF, put_in)
        take_matrix(flat, mat, FF, D, put_out)
        bias_in[...] = take_vector(flat, 2 * mat, FF)
        for i in range(3):
            vec[i : i + 1, :] = take_vector(flat, 2 * mat + FF // LANES + i * (D // LANES), D)
        acc_in[...] = jnp.zeros_like(acc_in)
        acc_out[...] = jnp.zeros_like(acc_out)
        acc_bias[...] = jnp.zeros_like(acc_bias)
        acc_vec[...] = jnp.zeros_like(acc_vec)
        small_o[...] = jnp.zeros_like(small_o)

    @pl.when(chunk < nch[item])
    def _():
        n2, r2 = norm_stats(h_ref[0])
        x2 = n2 * vec2_ref[3:4, :] + vec2_ref[4:5, :]
        x2b = x2.astype(bf16)
        u = dot(x2b, w_in[...]) + bias_in[...]
        cdf = 0.5 * (1.0 + lax.erf(u * 0.7071067811865476))
        f_sc[...] = (u * cdf).astype(bf16)
        gp_sc[...] = cdf + u * jnp.exp(u * u * -0.5) * (1.0 / math.sqrt(2.0 * math.pi))
        h3 = x2 + dot(f_sc[...], w_out[...]) + vec[0:1, :]
        n3, r3 = norm_stats(h3)
        at = lax.broadcasted_iota(jnp.int32, (CH, 1), 0) + chunk * CH
        valid = (at < LABEL + horizon[item]).astype(f32)
        y_o[0] = ((n3 * vec[1:2, :] + vec[2:3, :]) * valid).astype(bf16)
        dy = ct_ref[0].astype(f32) * valid
        acc_vec[1:2, :] += col_sum(dy * n3)
        acc_vec[2:3, :] += col_sum(dy)
        dh3 = norm_back(dy, n3, r3, vec[1:2, :])
        acc_vec[0:1, :] += col_sum(dh3)
        e3 = dh3.astype(bf16)
        acc_out[...] += dot(e3.T, f_sc[...])
        du = dot_nt(e3, w_out[...]) * gp_sc[...]
        acc_bias[...] += col_sum(du)
        eu = du.astype(bf16)
        acc_in[...] += dot(x2b.T, eu)
        dx2 = dh3 + dot_nt(eu, w_in[...])
        small_o[3:4, :] += col_sum(dx2 * n2)
        small_o[4:5, :] += col_sum(dx2)
        dh2 = norm_back(dx2, n2, r2, vec2_ref[3:4, :])
        small_o[2:3, :] += col_sum(dh2)
        dh2_o[0] = dh2

    @pl.when(chunk >= nch[item])
    def _():
        y_o[0] = jnp.zeros((CH, D), bf16)

    @pl.when(last)
    def _():
        put_matrix(flat, 0, D, FF, lambda j: acc_in[:, j * LANES : (j + 1) * LANES])
        for j in range(D // LANES):
            flat[pl.ds(mat + j, FF, stride=D // LANES), :] = acc_out[j * LANES : (j + 1) * LANES, :].T
        flat[2 * mat :, :] = jnp.zeros((flat.shape[0] - 2 * mat, LANES), f32)
        put_vector(flat, 2 * mat, acc_bias[...])
        for i in range(3):
            put_vector(flat, 2 * mat + FF // LANES + i * (D // LANES), acc_vec[i : i + 1, :])
        store_flat(order, gn_o, gf_o, flat, real)


def dense_both(nch, order, horizon, h2, ct, params, vec2, real):
    items, steps, _ = h2.shape
    chunks = steps // CH
    half, rows, _ = params[0].shape

    def row_block(i, c, nch_ref, _):
        return (i, jnp.minimum(c, nch_ref[i] - 1), 0)

    rowspec = pl.BlockSpec((1, CH, D), row_block)
    whole2 = lambda i, c, *_: (0, 0)
    shards = pl.BlockSpec((half, rows, LANES), lambda i, c, *_: (0, 0, 0), pipeline_mode=pl.Buffered(1))
    shape = jax.ShapeDtypeStruct
    return pl.pallas_call(
        functools.partial(dense_kernel, real=real),
        grid_spec=pltpu.PrefetchScalarGridSpec(
            num_scalar_prefetch=2,
            grid=(items, chunks),
            in_specs=[
                pl.BlockSpec(memory_space=pltpu.SMEM),
                rowspec, rowspec,
                shards, shards,
                pl.BlockSpec((8, D), whole2, pipeline_mode=pl.Buffered(1)),
            ],
            out_specs=[
                pl.BlockSpec((1, CH, D), lambda i, c, *_: (i, c, 0)),
                rowspec,
                shards, shards,
                pl.BlockSpec((8, D), whole2, pipeline_mode=pl.Buffered(1)),
            ],
            scratch_shapes=[
                pltpu.VMEM((2 * half * real + 16, LANES), f32),
                pltpu.VMEM((D, FF), bf16), pltpu.VMEM((FF, D), bf16),
                pltpu.VMEM((1, FF), f32), pltpu.VMEM((8, D), f32),
                pltpu.VMEM((D, FF), f32), pltpu.VMEM((D, FF), f32),
                pltpu.VMEM((1, FF), f32), pltpu.VMEM((8, D), f32),
                pltpu.VMEM((CH, FF), bf16), pltpu.VMEM((CH, FF), f32),
            ],
        ),
        out_shape=[
            shape((items, steps, D), bf16), shape((items, steps, D), f32),
            shape((half, rows, LANES), bf16), shape((half, rows, LANES), bf16), shape((8, D), f32),
        ],
        compiler_params=pltpu.CompilerParams(vmem_limit_bytes=VMEM_LIMIT),
        cost_estimate=pl.CostEstimate(flops=int(2e10), bytes_accessed=int(3e7), transcendentals=0),
        name="dense_both",
    )(nch, order, horizon, h2, ct, *params, vec2)


def attend_back(head, pair, keys_pair, values_pair, keys_t, qt, dat, q_pair, da_pair, lse, shift, scale, masks, causal):
    raw = dot(keys_pair, head_rhs(qt, head))
    s = raw * scale - lse
    if shift is not None:
        s = s + shift
    weights = jnp.exp2(s)
    if causal:
        weights = causal_cut(weights, 0.0)
    dp = dot(values_pair, head_rhs(dat, head))
    inner = jnp.sum(weights * dp, 0, keepdims=True)
    g = (weights * (dp - inner)).astype(bf16)
    mask = masks[head % 2]
    dv = dot(weights.astype(bf16), da_pair * mask)
    dk = dot(g, q_pair * mask)
    dqt = dot(keys_t, g)
    return dqt, dk, dv


def cross_backward_kernel(
    nch, order, tau, dh2_ref, h1_ref, m_ref, shift_ref, q_ref, qt_ref, k_ref, kt_ref, v_ref, at_ref, lse_ref,
    w, vec1_ref, small2_ref, dh1_o, gm_o, gn_o, gf_o, small_o,
    flat, acc, acc_vec, dksc, dvsc, dqt, *, real,
):
    item, chunk = pl.program_id(0), pl.program_id(1)
    first = (item == 0) & (chunk == 0)
    last = (item == pl.num_programs(0) - 1) & (chunk == pl.num_programs(1) - 1)

    @pl.when(first)
    def _():
        acc[...] = jnp.zeros_like(acc)
        acc_vec[...] = small2_ref[...]
        small_o[...] = jnp.zeros_like(small_o)

    @pl.when(chunk == 0)
    def _():
        dksc[...] = jnp.zeros_like(dksc)
        dvsc[...] = jnp.zeros_like(dvsc)

    @pl.when(chunk < nch[item])
    def _():
        factor = tau[item] * (1.0 / math.sqrt(HW))
        scale = tau[item] * (LOG2E / math.sqrt(HW))
        shift = shift_ref[0] * (LOG2E / math.sqrt(HW))
        dh2 = dh2_ref[0]
        e2 = dh2.astype(bf16)
        acc[:, 3 * D :] += dot(at_ref[0], e2)
        da = dot_nt(e2, w[:, 3 * D :]).astype(bf16)
        dat = da.T
        qt = qt_ref[0]
        masks = pair_masks((CH, LANES), bf16)
        for pair in range(HEADS // 2):
            lanes = slice(pair * LANES, (pair + 1) * LANES)
            dk_pair, dv_pair = 0.0, 0.0
            for head in (2 * pair, 2 * pair + 1):
                rows = slice(head * HW, (head + 1) * HW)
                part, dk, dv = attend_back(
                    head, pair, k_ref[0, :, lanes], v_ref[0, :, lanes], kt_ref[0, rows, :], qt, dat,
                    q_ref[0, :, lanes], da[:, lanes], lse_ref[0, head : head + 1, :], shift, scale, masks, False,
                )
                dqt[rows, :] = (part * factor).astype(bf16)
                dk_pair, dv_pair = dk_pair + dk, dv_pair + dv
            dksc[:, lanes] += dk_pair * factor
            dvsc[:, lanes] += dv_pair
        dq = dqt[...].T
        acc_vec[0:1, :] += col_sum(dq.astype(f32))
        n1, r1 = norm_stats(h1_ref[0])
        x1b = (n1 * vec1_ref[3:4, :] + vec1_ref[4:5, :]).astype(bf16)
        acc[:, :D] += dot(x1b.T, dq)
        dx1 = dh2 + dot_nt(dq, w[:, :D])
        small_o[3:4, :] += col_sum(dx1 * n1)
        small_o[4:5, :] += col_sum(dx1)
        dh1 = norm_back(dx1, n1, r1, vec1_ref[3:4, :])
        small_o[2:3, :] += col_sum(dh1)
        dh1_o[0] = dh1

    @pl.when(chunk == pl.num_programs(1) - 1)
    def _():
        dv = dvsc[...]
        acc_vec[1:2, :] += col_sum(dv)
        dkv = jnp.concatenate([dksc[...].astype(bf16), dv.astype(bf16)], 1)
        acc[:, D : 3 * D] += dot(m_ref[0].T, dkv)
        gm_o[0] = dot_nt(dkv, w[:, D : 3 * D])

    @pl.when(last)
    def _():
        store_attention(order, gn_o, gf_o, flat, real, acc, acc_vec)


def cross_backward(nch, order, tau, dh2, h1, memory, shift, saved, w, vec1, small2, half, rows, real):
    q, qt, k, kt, v, at, lse = saved
    items, steps, _ = h1.shape
    mem = memory.shape[1]
    chunks = steps // CH

    def row_block(i, c, nch_ref, _):
        return (i, jnp.minimum(c, nch_ref[i] - 1), 0)

    def col_block(i, c, nch_ref, _):
        return (i, 0, jnp.minimum(c, nch_ref[i] - 1))

    per_item = lambda i, c, *_: (i, 0, 0)
    rowspec = pl.BlockSpec((1, CH, D), row_block)
    colspec = pl.BlockSpec((1, D, CH), col_block)
    memspec = pl.BlockSpec((1, mem, D), per_item)
    whole2 = lambda i, c, *_: (0, 0)
    shards = pl.BlockSpec((half, rows, LANES), lambda i, c, *_: (0, 0, 0), pipeline_mode=pl.Buffered(1))
    once = pl.Buffered(1)
    shape = jax.ShapeDtypeStruct
    return pl.pallas_call(
        functools.partial(cross_backward_kernel, real=real),
        grid_spec=pltpu.PrefetchScalarGridSpec(
            num_scalar_prefetch=2,
            grid=(items, chunks),
            in_specs=[
                pl.BlockSpec(memory_space=pltpu.SMEM),
                rowspec, rowspec, memspec,
                pl.BlockSpec((1, mem, 1), per_item),
                rowspec, colspec, memspec,
                pl.BlockSpec((1, D, mem), per_item),
                memspec, colspec,
                pl.BlockSpec((1, HEADS, CH), col_block),
                pl.BlockSpec((D, 4 * D), whole2, pipeline_mode=once),
                pl.BlockSpec((8, D), whole2, pipeline_mode=once),
                pl.BlockSpec((8, D), whole2, pipeline_mode=once),
            ],
            out_specs=[
                rowspec, memspec,
                shards, shards,
                pl.BlockSpec((8, D), whole2, pipeline_mode=once),
            ],
            scratch_shapes=[
                pltpu.VMEM((2 * half * real + 16, LANES), f32),
                pltpu.VMEM((D, 4 * D), f32), pltpu.VMEM((8, D), f32),
                pltpu.VMEM((mem, D), f32), pltpu.VMEM((mem, D), f32),
                pltpu.VMEM((D, CH), bf16),
            ],
        ),
        out_shape=[
            shape((items, steps, D), f32), shape((items, mem, D), f32),
            shape((half, rows, LANES), bf16), shape((half, rows, LANES), bf16), shape((8, D), f32),
        ],
        compiler_params=pltpu.CompilerParams(vmem_limit_bytes=VMEM_LIMIT),
        cost_estimate=pl.CostEstimate(flops=int(8e9), bytes_accessed=int(2e7), transcendentals=0),
        name="cross_backward",
    )(nch, order, tau, dh2, h1, memory, shift, q, qt, k, kt, v, at, lse, w, vec1, small2)


def self_backward_kernel(
    nch, order, tau, dh1_ref, x_ref, q_ref, qt_ref, k_ref, kt_ref, v_ref, at_ref, lse_ref,
    w, small1_ref, gx_o, gn_o, gf_o,
    flat, acc, acc_vec, dksc, dvsc, dqt, *, real, chunks,
):
    item, step = pl.program_id(0), pl.program_id(1)
    chunk = chunks - 1 - step
    first = (item == 0) & (step == 0)
    last = (item == pl.num_programs(0) - 1) & (step == chunks - 1)

    @pl.when(first)
    def _():
        acc[...] = jnp.zeros_like(acc)
        acc_vec[...] = small1_ref[...]

    @pl.when(step == 0)
    def _():
        dksc[...] = jnp.zeros_like(dksc)
        dvsc[...] = jnp.zeros_like(dvsc)

    @pl.when(chunk < nch[item])
    def _():
        factor = tau[item] * (1.0 / math.sqrt(HW))
        scale = tau[item] * (LOG2E / math.sqrt(HW))
        dh1 = dh1_ref[0]
        e1 = dh1.astype(bf16)
        acc[:, 3 * D :] += dot(at_ref[0], e1)
        da = dot_nt(e1, w[:, 3 * D :]).astype(bf16)
        dat = da.T
        qt = qt_ref[0]
        masks = pair_masks((CH, LANES), bf16)
        for at_chunk in range(chunks):

            @pl.when(chunk == at_chunk)
            def _(keys=(at_chunk + 1) * CH):
                for pair in range(HEADS // 2):
                    lanes = slice(pair * LANES, (pair + 1) * LANES)
                    dk_pair, dv_pair = 0.0, 0.0
                    for head in (2 * pair, 2 * pair + 1):
                        rows = slice(head * HW, (head + 1) * HW)
                        part, dk, dv = attend_back(
                            head, pair, k_ref[0, :keys, lanes], v_ref[0, :keys, lanes], kt_ref[0, rows, :keys], qt, dat,
                            q_ref[0, :, lanes], da[:, lanes], lse_ref[0, head : head + 1, :], None, scale, masks, True,
                        )
                        dqt[rows, :] = (part * factor).astype(bf16)
                        dk_pair, dv_pair = dk_pair + dk, dv_pair + dv
                    dksc[:keys, lanes] += dk_pair * factor
                    dvsc[:keys, lanes] += dv_pair

        here = pl.ds(pl.multiple_of(chunk * CH, CH), CH)
        dq = dqt[...].T
        dv = dvsc[here, :]
        acc_vec[0:1, :] += col_sum(dq.astype(f32))
        acc_vec[1:2, :] += col_sum(dv)
        dqkv = jnp.concatenate([dq, dksc[here, :].astype(bf16), dv.astype(bf16)], 1)
        acc[:, : 3 * D] += dot(x_ref[0].T, dqkv)
        gx_o[0] = dh1 + dot_nt(dqkv, w[:, : 3 * D])

    @pl.when(chunk >= nch[item])
    def _():
        gx_o[0] = jnp.zeros((CH, D), f32)

    @pl.when(last)
    def _():
        store_attention(order, gn_o, gf_o, flat, real, acc, acc_vec)


def self_backward(nch, order, tau, dh1, x, saved, w, small1, half, rows, real):
    q, qt, k, kt, v, at, lse = saved
    items, steps, _ = x.shape
    chunks = steps // CH

    def row_block(i, c, nch_ref, _):
        return (i, jnp.minimum(chunks - 1 - c, nch_ref[i] - 1), 0)

    def col_block(i, c, nch_ref, _):
        return (i, 0, jnp.minimum(chunks - 1 - c, nch_ref[i] - 1))

    per_item = lambda i, c, *_: (i, 0, 0)
    rowspec = pl.BlockSpec((1, CH, D), row_block)
    colspec = pl.BlockSpec((1, D, CH), col_block)
    itemspec = pl.BlockSpec((1, steps, D), per_item)
    whole2 = lambda i, c, *_: (0, 0)
    shards = pl.BlockSpec((half, rows, LANES), lambda i, c, *_: (0, 0, 0), pipeline_mode=pl.Buffered(1))
    once = pl.Buffered(1)
    shape = jax.ShapeDtypeStruct
    return pl.pallas_call(
        functools.partial(self_backward_kernel, real=real, chunks=chunks),
        grid_spec=pltpu.PrefetchScalarGridSpec(
            num_scalar_prefetch=2,
            grid=(items, chunks),
            in_specs=[
                pl.BlockSpec(memory_space=pltpu.SMEM),
                rowspec, rowspec, rowspec, colspec, itemspec,
                pl.BlockSpec((1, D, steps), per_item),
                itemspec, colspec,
                pl.BlockSpec((1, HEADS, CH), col_block),
                pl.BlockSpec((D, 4 * D), whole2, pipeline_mode=once),
                pl.BlockSpec((8, D), whole2, pipeline_mode=once),
            ],
            out_specs=[
                pl.BlockSpec((1, CH, D), lambda i, c, *_: (i, chunks - 1 - c, 0)),
                shards, shards,
            ],
            scratch_shapes=[
                pltpu.VMEM((2 * half * real + 16, LANES), f32),
                pltpu.VMEM((D, 4 * D), f32), pltpu.VMEM((8, D), f32),
                pltpu.VMEM((steps, D), f32), pltpu.VMEM((steps, D), f32),
                pltpu.VMEM((D, CH), bf16),
            ],
        ),
        out_shape=[shape((items, steps, D), f32), shape((half, rows, LANES), bf16), shape((half, rows, LANES), bf16)],
        compiler_params=pltpu.CompilerParams(vmem_limit_bytes=VMEM_LIMIT),
        cost_estimate=pl.CostEstimate(flops=int(1.5e10), bytes_accessed=int(2e7), transcendentals=0),
        name="self_backward",
    )(nch, order, tau, dh1, x, q, qt, k, kt, v, at, lse, w, small1)


AXES = ("wide", "narrow")


def exchange(rows, offset, count):
    return lax.ppermute(rows, AXES, [(i, i ^ offset) for i in range(count)])


def offsets(narrow, count):
    core, plane = narrow, 4 * narrow
    along_z = list(range(plane, count, plane))
    within = [y * 2 * narrow + x for y in range(2) for x in range(narrow)][1:]
    return along_z, within, core


def slot_owners(narrow, count):
    along_z, within, core = offsets(narrow, count)
    near = [a ^ b for a in [0] + within for b in [0] + along_z]
    return near + [a ^ core for a in near]


def gather_shards(shard, narrow, count):
    along_z, within, core = offsets(narrow, count)
    line = jnp.stack([shard] + [exchange(shard, o, count) for o in along_z])
    near = jnp.concatenate([line] + [exchange(line, o, count) for o in within])
    return near, exchange(near, core, count)


def add_up(parts):
    return sum(part.astype(f32) for part in parts)


def scatter_shards(near, far, narrow, count):
    along_z, within, core = offsets(narrow, count)
    depth = 1 + len(along_z)
    mine = add_up([near, exchange(far, core, count)]).astype(bf16)
    got = [exchange(mine[(1 + i) * depth : (2 + i) * depth], o, count) for i, o in enumerate(within)]
    line = add_up([mine[:depth]] + got).astype(bf16)
    got = [exchange(line[1 + i], o, count) for i, o in enumerate(along_z)]
    return add_up([line[0]] + got)


def to_rows(shard):
    real = shard.shape[0] // LANES
    padded = (real + 15) // 16 * 16
    return jnp.pad(shard.reshape(real, LANES), ((0, padded - real), (0, 0)))


def from_rows(rows, length):
    return rows[: length // LANES].reshape(length)


def body(inputs, memory, tau_scale, delta_shift, horizon, self_params, cross_params, dense_params, cotangent):
    narrow = lax.axis_size("narrow")
    count = lax.axis_size(AXES)
    x, m, ct = inputs[:, 0], memory[:, 0], cotangent[:, 0]
    tau, shift, horizon = tau_scale[:, 0], delta_shift[:, 0, :, None], horizon[:, 0]
    order = lax.axis_index(AXES) ^ jnp.array(slot_owners(narrow, count), jnp.int32)
    steps = x.shape[1]
    nch = jnp.minimum((horizon + (LABEL + CH - 1)) // CH, steps // CH).astype(jnp.int32)
    real_a, real_d = self_params.shape[0] // LANES, dense_params.shape[0] // LANES
    p_self = gather_shards(to_rows(self_params), narrow, count)
    p_cross = gather_shards(to_rows(cross_params), narrow, count)
    p_dense = gather_shards(to_rows(dense_params), narrow, count)
    half, rows = p_self[0].shape[:2]
    q, qt, k, kt, v, at, h1, lse, w1, vec1 = self_forward(nch, order, tau, x, p_self, real_a)
    q2, qt2, k2, kt2, v2, at2, h2, lse2, w2, vec2 = cross_forward(nch, order, tau, h1, m, shift, p_cross, vec1, real_a)
    y, dh2, gn, gf, small2 = dense_both(nch, order, horizon, h2, ct, p_dense, vec2, real_d)
    g_dense = scatter_shards(gn, gf, narrow, count)
    dh1, gm, gn, gf, small1 = cross_backward(
        nch, order, tau, dh2, h1, m, shift, (q2, qt2, k2, kt2, v2, at2, lse2), w2, vec1, small2, half, rows, real_a
    )
    g_cross = scatter_shards(gn, gf, narrow, count)
    gx, gn, gf = self_backward(nch, order, tau, dh1, x, (q, qt, k, kt, v, at, lse), w1, small1, half, rows, real_a)
    g_self = scatter_shards(gn, gf, narrow, count)
    return (
        y[:, None], gx[:, None], gm[:, None],
        from_rows(g_self, self_params.shape[0]),
        from_rows(g_cross, cross_params.shape[0]),
        from_rows(g_dense, dense_params.shape[0]),
    )


def solution(mesh):
    items = P(None, AXES, None, None)
    placed = (items, items, P(None, AXES), P(None, AXES, None), P(None, AXES), P(AXES), P(AXES), P(AXES), items)
    return jax.shard_map(
        body, mesh=mesh, in_specs=placed, out_specs=(items, items, items, P(AXES), P(AXES), P(AXES)), check_vma=False
    )
```

time: 1190 us -> 332 us (0.28)
  matrix products: 432 us -> 0 us
  waiting for transfers between devices: 354 us -> 86.2 us
  local copies, waits for them, and re-layouts: 248 us -> 13.6 us
  Pallas kernels: 0 us -> 123 us
  other arithmetic: 120 us -> 6.33 us
  starting transfers between devices: 0.16 us -> 99.5 us
  between operations: 18.9 us -> 1.29 us
    dot_general x396 -> x0, matrix products: 432 us -> none  [the longest x96 136 us: head_scores(): jnp.einsum('ise,ime->ism', head_query, head_key, preferred_element_type=j...]
    unnamed x5 -> x0, waiting for transfers between devices: 264 us -> none
    pallas_call x0 -> x5, Pallas kernels: none -> 123 us  [the longest x1 33.4 us: dense_both(): pl.pallas_call(functools.partial(dense_kernel, real=real), grid_spec=pltp...]
    ppermute x0 -> x42, starting transfers between devices: none -> 99.5 us  [exchange(): return lax.ppermute(rows, AXES, [(i, i ^ offset) for i in range(count)])]
    all_gather x3 -> x0, waiting for transfers between devices: 89.8 us -> none  [the longest x1 49.1 us: body(): lax.all_gather(self_params, ('wide', 'narrow'), axis=0, tiled=True)]
    ppermute x0 -> x42, waiting for transfers between devices: none -> 86.2 us  [exchange(): return lax.ppermute(rows, AXES, [(i, i ^ offset) for i in range(count)])]
    unnamed x382 -> x42, local copies, waits for them, and re-layouts: 84.5 us -> 9.79 us
    squeeze x80 -> x3, local copies, waits for them, and re-layouts: 61.8 us -> 0.08 us  [scatter_shards(): got = [exchange(line[1 + i], o, count) for i, o in enumerate(along_z)]]
  transfers between devices with their start and end apart: 4 -> 42, of which waited for: 3 -> 20; matrix products, arithmetic and copies ran while one was open for 22% -> 5% of each run, Pallas kernels for 0% -> 12%
where the time goes in v1:
time: 332 us; the launch traced here: 330 us
  Pallas kernels  123 us (37%)
  starting transfers between devices  99.5 us (30%)
  waiting for transfers between devices  86.2 us (26%)
  local copies, waits for them, and re-layouts  13.6 us (4%)
  other arithmetic  6.33 us (2%)
    ppermute x42, starting transfers between devices, exchange(): return lax.ppermute(rows, AXES, [(i, i ^ offset) for i in range(count)])  99.5 us
    ppermute x42, waiting for transfers between devices, exchange(): return lax.ppermute(rows, AXES, [(i, i ^ offset) for i in range(count)])  86.2 us
    pallas_call x1, Pallas kernels, dense_both(): pl.pallas_call(functools.partial(dense_kernel, real=real), grid_spec=pltp...  33.4 us
    pallas_call x1, Pallas kernels, self_backward(): pl.pallas_call(functools.partial(self_backward_kernel, real=real, chunks=...  30.1 us
    pallas_call x1, Pallas kernels, self_forward(): pl.pallas_call(functools.partial(self_forward_kernel, real=real, chunks=c...  22.3 us
    pallas_call x1, Pallas kernels, cross_backward(): pl.pallas_call(functools.partial(cross_backward_kernel, real=real), grid_...  19.9 us
    pallas_call x1, Pallas kernels, cross_forward(): pl.pallas_call(functools.partial(cross_forward_kernel, real=real, mem=mem...  17.3 us
    unnamed x42, local copies, waits for them, and re-layouts  9.79 us
  transfers between devices with their start and end apart: 42, of which 20 were waited for; matrix products, arithmetic and copies ran while one was open for 5% of the time, Pallas kernels for 12%

profile of v1, /device:TPU:0, one launch (start us, length us, event | category | flops | bytes accessed | tf_op | source)
XLA Modules:
  0.0 330.1 jit_solution(1807790020250735203)
XLA Ops:
  0.7 1.0 pad_bitcast_fusion.2
  1.6 4.1 %collective-permute-start.15 = (bf16[528,128]{1,0:T(8,128)(2,1)S(1)}, bf16[528,128]{1,0:T(8,128)(2,1)S(1)}, u32[]{:S(2)}, u32[]{:S(2)}) collective-permute-start(bf16[528,128]{1,0:T(8,128)(2,1)S(1)} %get-tuple-element.106), channel_id=1, source_target_pairs={{0,16},{1,17},{2,18},{3,19},{4,20},{5,21},{6,22},{7,23},{8,24},{9,... | collective-permute-start | bytes 405512 | tf_op jit(solution)/shard_map/ppermute | solution.py:743
  5.7 1.6 collective-permute-start.14
  7.3 1.0 pad_bitcast_fusion
  8.3 2.0 collective-permute-start.1
  10.2 2.5 collective-permute-start
  12.7 1.5 constant_dynamic-update-slice_fusion.6
  14.2 0.9 constant_dynamic-update-slice_fusion.20
  17.4 2.7 collective-permute-start.2
  20.7 1.1 collective-permute-done.1
  22.6 1.0 collective-permute-done.2
  23.5 4.6 %collective-permute-start.7 = (bf16[272,128]{1,0:T(8,128)(2,1)S(1)}, bf16[272,128]{1,0:T(8,128)(2,1)S(1)}, u32[]{:S(2)}, u32[]{:S(2)}) collective-permute-start(bf16[272,128]{1,0:T(8,128)(2,1)S(1)} %get-tuple-element.108), channel_id=1, source_target_pairs={{0,8},{1,9},{2,10},{3,11},{4,12},{5,13},{6,14},{7,15},{8,0},{9,1},... | collective-permute-start | bytes 208904 | tf_op jit(solution)/shard_map/ppermute | solution.py:743
  28.8 1.6 collective-permute-done.7
  30.4 2.9 collective-permute-start.9
  34.0 2.5 collective-permute-start.5
  36.6 1.5 collective-permute-start.4
  38.2 1.6 collective-permute-start.3
  41.0 9.6 %collective-permute-done.3 = bf16[4,272,128]{2,1,0:T(8,128)(2,1)S(1)} collective-permute-done((bf16[4,272,128]{2,1,0:T(8,128)(2,1)S(1)}, bf16[4,272,128]{2,1,0:T(8,128)(2,1)S(1)}, u32[]{:S(2)}, u32[]{:S(2)}) %collective-permute-start.3) | collective-permute-done | bytes 278560 | tf_op jit(solution)/shard_map/ppermute | solution.py:743
  50.6 1.4 collective-permute-start.19
  52.1 1.6 collective-permute-start.12
  54.3 7.9 %collective-permute-done.17 = bf16[4,528,128]{2,1,0:T(8,128)(2,1)S(1)} collective-permute-done((bf16[4,528,128]{2,1,0:T(8,128)(2,1)S(1)}, bf16[4,528,128]{2,1,0:T(8,128)(2,1)S(1)}, u32[]{:S(2)}, u32[]{:S(2)}) %collective-permute-start.17) | collective-permute-done | bytes 540704 | tf_op jit(solution)/shard_map/ppermute | solution.py:743
  62.2 1.5 collective-permute-start.10
  63.9 9.9 %collective-permute-done.19 = bf16[4,528,128]{2,1,0:T(8,128)(2,1)S(1)} collective-permute-done((bf16[4,528,128]{2,1,0:T(8,128)(2,1)S(1)}, bf16[4,528,128]{2,1,0:T(8,128)(2,1)S(1)}, u32[]{:S(2)}, u32[]{:S(2)}) %collective-permute-start.19) | collective-permute-done | bytes 540704 | tf_op jit(solution)/shard_map/ppermute | solution.py:743
  75.4 9.1 %collective-permute-done.10 = bf16[4,272,128]{2,1,0:T(8,128)(2,1)S(1)} collective-permute-done((bf16[4,272,128]{2,1,0:T(8,128)(2,1)S(1)}, bf16[4,272,128]{2,1,0:T(8,128)(2,1)S(1)}, u32[]{:S(2)}, u32[]{:S(2)}) %collective-permute-start.10) | collective-permute-done | bytes 278560 | tf_op jit(solution)/shard_map/ppermute | solution.py:743
  87.7 1.0 copy-done.9
  88.7 22.3 %self_forward.1 = (bf16[2,768,512]{2,1,0:T(8,128)(2,1)}, bf16[2,512,768]{2,1,0:T(8,128)(2,1)}, bf16[2,768,512]{2,1,0:T(8,128)(2,1)}, bf16[2,512,768]{2,1,0:T(8,1...) custom-call(s32[2]{0:T(128)} %fusion.9.nch, ...), custom_call_target="tpu_custom_call" | custom-call | flops 8000000000 | bytes 20000000 | tf_op jit(solution)/shard_map/self_forward/pallas_call | solution.py:200
  111.0 17.3 %cross_forward.1 = (bf16[2,768,512]{2,1,0:T(8,128)(2,1)}, bf16[2,512,768]{2,1,0:T(8,128)(2,1)}, bf16[2,96,512]{2,1,0:T(8,128)(2,1)}, bf16[2,512,96]{2,1,0:T(8,12...) custom-call(s32[2]{0:T(128)} %fusion.9.nch, ...), custom_call_target="tpu_custom_call" | custom-call | flops 4000000000 | bytes 20000000 | tf_op jit(solution)/shard_map/cross_forward/pallas_call | solution.py:305
  128.4 33.4 %dense_both.1 = (bf16[2,768,512]{2,1,0:T(8,128)(2,1)}, f32[2,768,512]{2,1,0:T(8,128)}, bf16[16,528,128]{2,1,0:T(8,128)(2,1)}, bf16[16,528,128]{2,1,0:T(8,128)(2,1)}, f32[8,512]{1,0:T(8,128)}) custom-call(s32[2]{0:T(128)} %fusion.9.nch, s32[32]{0:T(128)} %broadcast_xor_fusion.order, s32[2]{0:T(128)} %bitcast.100, f32[2,768,512]{2,1,0:T(8,128)} %get-tuple-element.41.h_ref, ...), custom_call_target="tpu_custom_call" | custom-call | flops 20000000000 | bytes 30000000 | tf_op jit(solution)/shard_map/dense_both/pallas_call | solution.py:438
  161.8 19.9 %cross_backward.1 = (f32[2,768,512]{2,1,0:T(8,128)}, f32[2,96,512]{2,1,0:T(8,128)}, bf16[16,272,128]{2,1,0:T(8,128)(2,1)}, bf16[16,272,128]{2,1,0:T(8,128)(2,1)}, f32[8,512]{1,0:T(8,128)}) custom-call(s32[2]{0:T(128)} %fusion.9.nch, s32[32]{0:T(128)} %broadcast_xor_fusion.order, f32[2]{0:T(128)} %bitcast.103, f32[2,768,512]{2,1,0:T(8,128)} %get-tuple-element.44.dh2_ref, ...), custom_call_target="tpu_custom_call" | custom-call | flops 8000000000 | bytes 20000000 | tf_op jit(solution)/shard_map/cross_backward/pallas_call | solution.py:582
  181.7 30.1 %self_backward.1 = (f32[2,768,512]{2,1,0:T(8,128)}, bf16[16,272,128]{2,1,0:T(8,128)(2,1)}, bf16[16,272,128]{2,1,0:T(8,128)(2,1)}) custom-call(s32[2]{0:T(128)} %fusion.9.nch, s32[32]{0:T(128)} %broadcast_xor_fusion.order, f32[2]{0:T(128)} %bitcast.104, f32[2,768,512]{2,1,0:T(8,128)} %get-tuple-element.54.dh1_ref, bf16[2,768,512]{2,1,0:T(8,128)(2,1)} %bitcast.97, ...), custom_call_target="tpu_custom_call" | custom-call | flops 15000000512 | bytes 20000000 | tf_op jit(solution)/shard_map/self_backward/pallas_call | solution.py:707
  211.9 23.2 %collective-permute-start.21 = (bf16[16,272,128]{2,1,0:T(8,128)(2,1)}, bf16[16,272,128]{2,1,0:T(8,128)(2,1)S(1)}, u32[]{:S(2)}, u32[]{:S(2)}) collective-permute-start(bf16[16,272,128]{2,1,0:T(8,128)(2,1)} %get-tuple-element.67), channel_id=1, source_target_pairs={{0,2},{1,3},{2,0},{3,1},{4,6},{5,7},{6,4},{7,5},{8,10},{9,11},{10,... | collective-permute-start | bytes 3342344 | tf_op jit(solution)/shard_map/ppermute | solution.py:743
  235.5 2.8 collective-permute-done.21
  238.3 1.5 add_convert_fusion.2
  240.0 20.5 %collective-permute-start.24 = (bf16[4,272,128]{2,1,0:T(8,128)(2,1)S(1)}, bf16[4,272,128]{2,1,0:T(8,128)(2,1)S(1)}, u32[]{:S(2)}, u32[]{:S(2)}) collective-permute-start(bf16[4,272,128]{2,1,0:T(8,128)(2,1)S(1)} %get-tuple-element.91), channel_id=1, source_target_pairs={{0,5},{1,4},{2,7},{3,6},{4,1},{5,0},{6,3},{7,2},{8,13},{9,12},{10,... | collective-permute-start | bytes 835592 | tf_op jit(solution)/shard_map/ppermute | solution.py:743
  261.6 6.4 %collective-permute-start.31 = (bf16[4,272,128]{2,1,0:T(8,128)(2,1)S(1)}, bf16[4,272,128]{2,1,0:T(8,128)(2,1)S(1)}, u32[]{:S(2)}, u32[]{:S(2)}) collective-permute-start(bf16[4,272,128]{2,1,0:T(8,128)(2,1)S(1)} %get-tuple-element.88), channel_id=1, source_target_pairs={{0,5},{1,4},{2,7},{3,6},{4,1},{5,0},{6,3},{7,2},{8,13},{9,12},{10,... | collective-permute-start | bytes 835592 | tf_op jit(solution)/shard_map/ppermute | solution.py:743
  268.0 6.0 %collective-permute-done.24 = bf16[4,272,128]{2,1,0:T(8,128)(2,1)S(1)} collective-permute-done((bf16[4,272,128]{2,1,0:T(8,128)(2,1)S(1)}, bf16[4,272,128]{2,1,0:T(8,128)(2,1)S(1)}, u32[]{:S(2)}, u32[]{:S(2)}) %collective-permute-start.24) | collective-permute-done | bytes 278560 | tf_op jit(solution)/shard_map/ppermute | solution.py:743
  275.0 5.2 %collective-permute-start.27 = (bf16[272,128]{1,0:T(8,128)(2,1)S(1)}, bf16[272,128]{1,0:T(8,128)(2,1)S(1)}, u32[]{:S(2)}, u32[]{:S(2)}) collective-permute-start(bf16[272,128]{1,0:T(8,128)(2,1)S(1)} %get-tuple-element.102), channel_id=1, source_target_pairs={{0,24},{1,25},{2,26},{3,27},{4,28},{5,29},{6,30},{7,31},{8,16},{9,... | collective-permute-start | bytes 208904 | tf_op jit(solution)/shard_map/ppermute | solution.py:743
  280.2 5.1 %collective-permute-done.31 = bf16[4,272,128]{2,1,0:T(8,128)(2,1)S(1)} collective-permute-done((bf16[4,272,128]{2,1,0:T(8,128)(2,1)S(1)}, bf16[4,272,128]{2,1,0:T(8,128)(2,1)S(1)}, u32[]{:S(2)}, u32[]{:S(2)}) %collective-permute-start.31) | collective-permute-done | bytes 278560 | tf_op jit(solution)/shard_map/ppermute | solution.py:743
  285.3 1.8 collective-permute-done.30
  287.4 2.6 collective-permute-start.34
  291.3 2.9 collective-permute-start.37
  294.9 11.0 %collective-permute-done.36 = bf16[4,528,128]{2,1,0:T(8,128)(2,1)S(1)} collective-permute-done((bf16[4,528,128]{2,1,0:T(8,128)(2,1)S(1)}, bf16[4,528,128]{2,1,0:T(8,128)(2,1)S(1)}, u32[]{:S(2)}, u32[]{:S(2)}) %collective-permute-start.36) | collective-permute-done | bytes 540704 | tf_op jit(solution)/shard_map/ppermute | solution.py:743
  305.9 0.9 collective-permute-start.33
  306.8 6.3 %collective-permute-done.38 = bf16[4,528,128]{2,1,0:T(8,128)(2,1)S(1)} collective-permute-done((bf16[4,528,128]{2,1,0:T(8,128)(2,1)S(1)}, bf16[4,528,128]{2,1,0:T(8,128)(2,1)S(1)}, u32[]{:S(2)}, u32[]{:S(2)}) %collective-permute-start.38) | collective-permute-done | bytes 540704 | tf_op jit(solution)/shard_map/ppermute | solution.py:743
  313.1 3.0 collective-permute-done.37
  316.5 2.6 collective-permute-start.41
  321.5 2.7 collective-permute-done.41
  324.2 4.9 %collective-permute-done.40 = bf16[528,128]{1,0:T(8,128)(2,1)S(1)} collective-permute-done((bf16[528,128]{1,0:T(8,128)(2,1)S(1)}, bf16[528,128]{1,0:T(8,128)(2,1)S(1)}, u32[]{:S(2)}, u32[]{:S(2)}) %collective-permute-start.40) | collective-permute-done | bytes 135200 | tf_op jit(solution)/shard_map/ppermute | solution.py:743
  (109 shorter events, 20.3 us)
Async XLA Ops:
  0.6 15.3 %copy-start.2 = (bf16[32896]{0:T(1024)(128)(2,1)S(1)}, bf16[32896]{0:T(1024)(128)(2,1)}, u32[]{:S(2)}) copy-start(bf16[32896]{0:T(1024)(128)(2,1)} %param.16) | copy-start | bytes 197380
  1.6 36.5 %collective-permute-start.15 = (bf16[528,128]{1,0:T(8,128)(2,1)S(1)}, bf16[528,128]{1,0:T(8,128)(2,1)S(1)}, u32[]{:S(2)}, u32[]{:S(2)}) collective-permute-start(bf16[528,128]{1,0:T(8,128)(2,1)S(1)} %get-tuple-element.106), channel_id=1, source_target_pairs={{0,16},{1,17},{2,18},{3,19},{4,20},{5,21},{6,22},{7,23},{8,24},{9,... | collective-permute-start | bytes 405512 | tf_op jit(solution)/shard_map/ppermute | solution.py:743
  5.7 34.0 %collective-permute-start.14 = (bf16[528,128]{1,0:T(8,128)(2,1)S(1)}, bf16[528,128]{1,0:T(8,128)(2,1)S(1)}, u32[]{:S(2)}, u32[]{:S(2)}) collective-permute-start(bf16[528,128]{1,0:T(8,128)(2,1)S(1)} %get-tuple-element.106), channel_id=1, source_target_pairs={{0,8},{1,9},{2,10},{3,11},{4,12},{5,13},{6,14},{7,15},{8,0},{9,1},... | collective-permute-start | bytes 405512 | tf_op jit(solution)/shard_map/ppermute | solution.py:743
  7.3 32.4 %collective-permute-start.16 = (bf16[528,128]{1,0:T(8,128)(2,1)S(1)}, bf16[528,128]{1,0:T(8,128)(2,1)S(1)}, u32[]{:S(2)}, u32[]{:S(2)}) collective-permute-start(bf16[528,128]{1,0:T(8,128)(2,1)S(1)} %get-tuple-element.106), channel_id=1, source_target_pairs={{0,24},{1,25},{2,26},{3,27},{4,28},{5,29},{6,30},{7,31},{8,16},{9,... | collective-permute-start | bytes 405512 | tf_op jit(solution)/shard_map/ppermute | solution.py:743
  8.3 13.6 %collective-permute-start.1 = (bf16[272,128]{1,0:T(8,128)(2,1)S(1)}, bf16[272,128]{1,0:T(8,128)(2,1)S(1)}, u32[]{:S(2)}, u32[]{:S(2)}) collective-permute-start(bf16[272,128]{1,0:T(8,128)(2,1)S(1)} %get-tuple-element.111), channel_id=1, source_target_pairs={{0,16},{1,17},{2,18},{3,19},{4,20},{5,21},{6,22},{7,23},{8,24},{9,... | collective-permute-start | bytes 208904 | tf_op jit(solution)/shard_map/ppermute | solution.py:743
  10.2 7.1 %collective-permute-start = (bf16[272,128]{1,0:T(8,128)(2,1)S(1)}, bf16[272,128]{1,0:T(8,128)(2,1)S(1)}, u32[]{:S(2)}, u32[]{:S(2)}) collective-permute-start(bf16[272,128]{1,0:T(8,128)(2,1)S(1)} %get-tuple-element.111), channel_id=1, source_target_pairs={{0,8},{1,9},{2,10},{3,11},{4,12},{5,13},{6,14},{7,15},{8,0},{9,1},... | collective-permute-start | bytes 208904 | tf_op jit(solution)/shard_map/ppermute | solution.py:743
  17.4 6.2 %collective-permute-start.2 = (bf16[272,128]{1,0:T(8,128)(2,1)S(1)}, bf16[272,128]{1,0:T(8,128)(2,1)S(1)}, u32[]{:S(2)}, u32[]{:S(2)}) collective-permute-start(bf16[272,128]{1,0:T(8,128)(2,1)S(1)} %get-tuple-element.111), channel_id=1, source_target_pairs={{0,24},{1,25},{2,26},{3,27},{4,28},{5,29},{6,30},{7,31},{8,16},{9,... | collective-permute-start | bytes 208904 | tf_op jit(solution)/shard_map/ppermute | solution.py:743
  21.8 12.1 %collective-permute-start.8 = (bf16[272,128]{1,0:T(8,128)(2,1)S(1)}, bf16[272,128]{1,0:T(8,128)(2,1)S(1)}, u32[]{:S(2)}, u32[]{:S(2)}) collective-permute-start(bf16[272,128]{1,0:T(8,128)(2,1)S(1)} %get-tuple-element.108), channel_id=1, source_target_pairs={{0,16},{1,17},{2,18},{3,19},{4,20},{5,21},{6,22},{7,23},{8,24},{9,... | collective-permute-start | bytes 208904 | tf_op jit(solution)/shard_map/ppermute | solution.py:743
  23.5 6.9 %collective-permute-start.7 = (bf16[272,128]{1,0:T(8,128)(2,1)S(1)}, bf16[272,128]{1,0:T(8,128)(2,1)S(1)}, u32[]{:S(2)}, u32[]{:S(2)}) collective-permute-start(bf16[272,128]{1,0:T(8,128)(2,1)S(1)} %get-tuple-element.108), channel_id=1, source_target_pairs={{0,8},{1,9},{2,10},{3,11},{4,12},{5,13},{6,14},{7,15},{8,0},{9,1},... | collective-permute-start | bytes 208904 | tf_op jit(solution)/shard_map/ppermute | solution.py:743
  30.4 6.2 %collective-permute-start.9 = (bf16[272,128]{1,0:T(8,128)(2,1)S(1)}, bf16[272,128]{1,0:T(8,128)(2,1)S(1)}, u32[]{:S(2)}, u32[]{:S(2)}) collective-permute-start(bf16[272,128]{1,0:T(8,128)(2,1)S(1)} %get-tuple-element.108), channel_id=1, source_target_pairs={{0,24},{1,25},{2,26},{3,27},{4,28},{5,29},{6,30},{7,31},{8,16},{9,... | collective-permute-start | bytes 208904 | tf_op jit(solution)/shard_map/ppermute | solution.py:743
  34.0 19.7 %collective-permute-start.5 = (bf16[4,272,128]{2,1,0:T(8,128)(2,1)S(1)}, bf16[4,272,128]{2,1,0:T(8,128)(2,1)S(1)}, u32[]{:S(2)}, u32[]{:S(2)}) collective-permute-start(bf16[4,272,128]{2,1,0:T(8,128)(2,1)S(1)} %pad_maximum_fusion.1), channel_id=1, source_target_pairs={{0,5},{1,4},{2,7},{3,6},{4,1},{5,0},{6,3},{7,2},{8,13},{9,12},{10,... | collective-permute-start | bytes 835592 | tf_op jit(solution)/shard_map/ppermute | solution.py:743
  36.6 15.4 %collective-permute-start.4 = (bf16[4,272,128]{2,1,0:T(8,128)(2,1)S(1)}, bf16[4,272,128]{2,1,0:T(8,128)(2,1)S(1)}, u32[]{:S(2)}, u32[]{:S(2)}) collective-permute-start(bf16[4,272,128]{2,1,0:T(8,128)(2,1)S(1)} %pad_maximum_fusion.1), channel_id=1, source_target_pairs={{0,4},{1,5},{2,6},{3,7},{4,0},{5,1},{6,2},{7,3},{8,12},{9,13},{10,... | collective-permute-start | bytes 835592 | tf_op jit(solution)/shard_map/ppermute | solution.py:743
  38.2 12.4 %collective-permute-start.3 = (bf16[4,272,128]{2,1,0:T(8,128)(2,1)S(1)}, bf16[4,272,128]{2,1,0:T(8,128)(2,1)S(1)}, u32[]{:S(2)}, u32[]{:S(2)}) collective-permute-start(bf16[4,272,128]{2,1,0:T(8,128)(2,1)S(1)} %pad_maximum_fusion.1), channel_id=1, source_target_pairs={{0,1},{1,0},{2,3},{3,2},{4,5},{5,4},{6,7},{7,6},{8,9},{9,8},{10,11... | collective-permute-start | bytes 835592 | tf_op jit(solution)/shard_map/ppermute | solution.py:743
  39.8 23.9 %collective-permute-start.18 = (bf16[4,528,128]{2,1,0:T(8,128)(2,1)S(1)}, bf16[4,528,128]{2,1,0:T(8,128)(2,1)S(1)}, u32[]{:S(2)}, u32[]{:S(2)}) collective-permute-start(bf16[4,528,128]{2,1,0:T(8,128)(2,1)S(1)} %pad_maximum_fusion), channel_id=1, source_target_pairs={{0,4},{1,5},{2,6},{3,7},{4,0},{5,1},{6,2},{7,3},{8,12},{9,13},{10,... | collective-permute-start | bytes 1622024 | tf_op jit(solution)/shard_map/ppermute | solution.py:743
  40.4 21.8 %collective-permute-start.17 = (bf16[4,528,128]{2,1,0:T(8,128)(2,1)S(1)}, bf16[4,528,128]{2,1,0:T(8,128)(2,1)S(1)}, u32[]{:S(2)}, u32[]{:S(2)}) collective-permute-start(bf16[4,528,128]{2,1,0:T(8,128)(2,1)S(1)} %pad_maximum_fusion), channel_id=1, source_target_pairs={{0,1},{1,0},{2,3},{3,2},{4,5},{5,4},{6,7},{7,6},{8,9},{9,8},{10,11... | collective-permute-start | bytes 1622024 | tf_op jit(solution)/shard_map/ppermute | solution.py:743
  50.6 23.2 %collective-permute-start.19 = (bf16[4,528,128]{2,1,0:T(8,128)(2,1)S(1)}, bf16[4,528,128]{2,1,0:T(8,128)(2,1)S(1)}, u32[]{:S(2)}, u32[]{:S(2)}) collective-permute-start(bf16[4,528,128]{2,1,0:T(8,128)(2,1)S(1)} %pad_maximum_fusion), channel_id=1, source_target_pairs={{0,5},{1,4},{2,7},{3,6},{4,1},{5,0},{6,3},{7,2},{8,13},{9,12},{10,... | collective-permute-start | bytes 1622024 | tf_op jit(solution)/shard_map/ppermute | solution.py:743
  52.1 33.9 %collective-permute-start.12 = (bf16[4,272,128]{2,1,0:T(8,128)(2,1)S(1)}, bf16[4,272,128]{2,1,0:T(8,128)(2,1)S(1)}, u32[]{:S(2)}, u32[]{:S(2)}) collective-permute-start(bf16[4,272,128]{2,1,0:T(8,128)(2,1)S(1)} %pad_maximum_fusion.2), channel_id=1, source_target_pairs={{0,5},{1,4},{2,7},{3,6},{4,1},{5,0},{6,3},{7,2},{8,13},{9,12},{10,... | collective-permute-start | bytes 835592 | tf_op jit(solution)/shard_map/ppermute | solution.py:743
  53.7 31.5 %collective-permute-start.11 = (bf16[4,272,128]{2,1,0:T(8,128)(2,1)S(1)}, bf16[4,272,128]{2,1,0:T(8,128)(2,1)S(1)}, u32[]{:S(2)}, u32[]{:S(2)}) collective-permute-start(bf16[4,272,128]{2,1,0:T(8,128)(2,1)S(1)} %pad_maximum_fusion.2), channel_id=1, source_target_pairs={{0,4},{1,5},{2,6},{3,7},{4,0},{5,1},{6,2},{7,3},{8,12},{9,13},{10,... | collective-permute-start | bytes 835592 | tf_op jit(solution)/shard_map/ppermute | solution.py:743
  54.3 19.6 %copy-start.5 = (bf16[16,272,128]{2,1,0:T(8,128)(2,1)}, bf16[16,272,128]{2,1,0:T(8,128)(2,1)S(1)}, u32[]{:S(2)}) copy-start(bf16[16,272,128]{2,1,0:T(8,128)(2,1)S(1)} %constant_dynamic-update-slice_fusion.pn_ref) | copy-start | bytes 3342340
  62.2 22.3 %collective-permute-start.10 = (bf16[4,272,128]{2,1,0:T(8,128)(2,1)S(1)}, bf16[4,272,128]{2,1,0:T(8,128)(2,1)S(1)}, u32[]{:S(2)}, u32[]{:S(2)}) collective-permute-start(bf16[4,272,128]{2,1,0:T(8,128)(2,1)S(1)} %pad_maximum_fusion.2), channel_id=1, source_target_pairs={{0,1},{1,0},{2,3},{3,2},{4,5},{5,4},{6,7},{7,6},{8,9},{9,8},{10,11... | collective-permute-start | bytes 835592 | tf_op jit(solution)/shard_map/ppermute | solution.py:743
  63.7 24.0 %collective-permute-start.6 = (bf16[16,272,128]{2,1,0:T(8,128)(2,1)S(1)}, bf16[16,272,128]{2,1,0:T(8,128)(2,1)S(1)}, u32[]{:S(2)}, u32[]{:S(2)}) collective-permute-start(bf16[16,272,128]{2,1,0:T(8,128)(2,1)S(1)} %constant_dynamic-update-slice_fusion.pn_ref), channel_id=1, source_target_pairs={{0,2},{1,3},{2,0},{3,1},{4,6},{5,7},{6,4},{7,5},{8,10},{9,11},{10,... | collective-permute-start | bytes 3342344 | tf_op jit(solution)/shard_map/ppermute | solution.py:743
  73.9 37.1 %copy-start.3 = (bf16[16,528,128]{2,1,0:T(8,128)(2,1)}, bf16[16,528,128]{2,1,0:T(8,128)(2,1)S(1)}, u32[]{:S(2)}) copy-start(bf16[16,528,128]{2,1,0:T(8,128)(2,1)S(1)} %constant_dynamic-update-slice_fusion.14.pn_ref) | copy-start | bytes 6488068
  73.9 54.5 %collective-permute-start.20 = (bf16[16,528,128]{2,1,0:T(8,128)(2,1)S(1)}, bf16[16,528,128]{2,1,0:T(8,128)(2,1)}, u32[]{:S(2)}, u32[]{:S(2)}) collective-permute-start(bf16[16,528,128]{2,1,0:T(8,128)(2,1)S(1)} %constant_dynamic-update-slice_fusion.14.pn_ref), channel_id=1, source_target_pairs={{0,2},{1,3},{2,0},{3,1},{4,6},{5,7},{6,4},{7,5},{8,10},{9,11},{10,... | collective-permute-start | bytes 6488072 | tf_op jit(solution)/shard_map/ppermute | solution.py:743
  86.7 24.3 %collective-permute-start.13 = (bf16[16,272,128]{2,1,0:T(8,128)(2,1)}, bf16[16,272,128]{2,1,0:T(8,128)(2,1)}, u32[]{:S(2)}, u32[]{:S(2)}) collective-permute-start(bf16[16,272,128]{2,1,0:T(8,128)(2,1)} %constant_dynamic-update-slice_fusion.7.pn_ref), channel_id=1, source_target_pairs={{0,2},{1,3},{2,0},{3,1},{4,6},{5,7},{6,4},{7,5},{8,10},{9,11},{10,... | collective-permute-start | bytes 3342344 | tf_op jit(solution)/shard_map/ppermute | solution.py:743
  181.7 53.3 %copy-start.8 = (bf16[16,272,128]{2,1,0:T(8,128)(2,1)S(1)}, bf16[16,272,128]{2,1,0:T(8,128)(2,1)}, u32[]{:S(2)}) copy-start(bf16[16,272,128]{2,1,0:T(8,128)(2,1)} %get-tuple-element.69) | copy-start | bytes 3342340
  181.7 53.4 %copy-start.7 = (bf16[16,528,128]{2,1,0:T(8,128)(2,1)S(1)}, bf16[16,528,128]{2,1,0:T(8,128)(2,1)}, u32[]{:S(2)}) copy-start(bf16[16,528,128]{2,1,0:T(8,128)(2,1)} %get-tuple-element.71) | copy-start | bytes 6488068
  211.9 26.5 %collective-permute-start.21 = (bf16[16,272,128]{2,1,0:T(8,128)(2,1)}, bf16[16,272,128]{2,1,0:T(8,128)(2,1)S(1)}, u32[]{:S(2)}, u32[]{:S(2)}) collective-permute-start(bf16[16,272,128]{2,1,0:T(8,128)(2,1)} %get-tuple-element.67), channel_id=1, source_target_pairs={{0,2},{1,3},{2,0},{3,1},{4,6},{5,7},{6,4},{7,5},{8,10},{9,11},{10,... | collective-permute-start | bytes 3342344 | tf_op jit(solution)/shard_map/ppermute | solution.py:743
  235.0 25.5 %collective-permute-start.28 = (bf16[16,272,128]{2,1,0:T(8,128)(2,1)S(1)}, bf16[16,272,128]{2,1,0:T(8,128)(2,1)S(1)}, u32[]{:S(2)}, u32[]{:S(2)}) collective-permute-start(bf16[16,272,128]{2,1,0:T(8,128)(2,1)S(1)} %copy-done.8), channel_id=1, source_target_pairs={{0,2},{1,3},{2,0},{3,1},{4,6},{5,7},{6,4},{7,5},{8,10},{9,11},{10,... | collective-permute-start | bytes 3342344 | tf_op jit(solution)/shard_map/ppermute | solution.py:743
  235.1 52.2 %collective-permute-start.35 = (bf16[16,528,128]{2,1,0:T(8,128)(2,1)S(1)}, bf16[16,528,128]{2,1,0:T(8,128)(2,1)S(1)}, u32[]{:S(2)}, u32[]{:S(2)}) collective-permute-start(bf16[16,528,128]{2,1,0:T(8,128)(2,1)S(1)} %copy-done.7), channel_id=1, source_target_pairs={{0,2},{1,3},{2,0},{3,1},{4,6},{5,7},{6,4},{7,5},{8,10},{9,11},{10,... | collective-permute-start | bytes 6488072 | tf_op jit(solution)/shard_map/ppermute | solution.py:743
  239.9 20.7 %copy-start.1 = (bf16[16,272,128]{2,1,0:T(8,128)(2,1)S(1)}, bf16[16,272,128]{2,1,0:T(8,128)(2,1)}, u32[]{:S(2)}) copy-start(bf16[16,272,128]{2,1,0:T(8,128)(2,1)} %get-tuple-element.68) | copy-start | bytes 3342340
  239.9 21.6 %collective-permute-start.22 = (bf16[4,272,128]{2,1,0:T(8,128)(2,1)S(1)}, bf16[4,272,128]{2,1,0:T(8,128)(2,1)S(1)}, u32[]{:S(2)}, u32[]{:S(2)}) collective-permute-start(bf16[4,272,128]{2,1,0:T(8,128)(2,1)S(1)} %get-tuple-element.90), channel_id=1, source_target_pairs={{0,1},{1,0},{2,3},{3,2},{4,5},{5,4},{6,7},{7,6},{8,9},{9,8},{10,11... | collective-permute-start | bytes 835592 | tf_op jit(solution)/shard_map/ppermute | solution.py:743
  240.0 34.0 %collective-permute-start.24 = (bf16[4,272,128]{2,1,0:T(8,128)(2,1)S(1)}, bf16[4,272,128]{2,1,0:T(8,128)(2,1)S(1)}, u32[]{:S(2)}, u32[]{:S(2)}) collective-permute-start(bf16[4,272,128]{2,1,0:T(8,128)(2,1)S(1)} %get-tuple-element.91), channel_id=1, source_target_pairs={{0,5},{1,4},{2,7},{3,6},{4,1},{5,0},{6,3},{7,2},{8,13},{9,12},{10,... | collective-permute-start | bytes 835592 | tf_op jit(solution)/shard_map/ppermute | solution.py:743
  260.6 14.1 %collective-permute-start.23 = (bf16[4,272,128]{2,1,0:T(8,128)(2,1)S(1)}, bf16[4,272,128]{2,1,0:T(8,128)(2,1)S(1)}, u32[]{:S(2)}, u32[]{:S(2)}) collective-permute-start(bf16[4,272,128]{2,1,0:T(8,128)(2,1)S(1)} %get-tuple-element.92), channel_id=1, source_target_pairs={{0,4},{1,5},{2,6},{3,7},{4,0},{5,1},{6,2},{7,3},{8,12},{9,13},{10,... | collective-permute-start | bytes 835592 | tf_op jit(solution)/shard_map/ppermute | solution.py:743
  260.9 14.0 %collective-permute-start.29 = (bf16[4,272,128]{2,1,0:T(8,128)(2,1)S(1)}, bf16[4,272,128]{2,1,0:T(8,128)(2,1)S(1)}, u32[]{:S(2)}, u32[]{:S(2)}) collective-permute-start(bf16[4,272,128]{2,1,0:T(8,128)(2,1)S(1)} %get-tuple-element.87), channel_id=1, source_target_pairs={{0,1},{1,0},{2,3},{3,2},{4,5},{5,4},{6,7},{7,6},{8,9},{9,8},{10,11... | collective-permute-start | bytes 835592 | tf_op jit(solution)/shard_map/ppermute | solution.py:743
  261.6 23.7 %collective-permute-start.31 = (bf16[4,272,128]{2,1,0:T(8,128)(2,1)S(1)}, bf16[4,272,128]{2,1,0:T(8,128)(2,1)S(1)}, u32[]{:S(2)}, u32[]{:S(2)}) collective-permute-start(bf16[4,272,128]{2,1,0:T(8,128)(2,1)S(1)} %get-tuple-element.88), channel_id=1, source_target_pairs={{0,5},{1,4},{2,7},{3,6},{4,1},{5,0},{6,3},{7,2},{8,13},{9,12},{10,... | collective-permute-start | bytes 835592 | tf_op jit(solution)/shard_map/ppermute | solution.py:743
  274.0 13.0 %collective-permute-start.30 = (bf16[4,272,128]{2,1,0:T(8,128)(2,1)S(1)}, bf16[4,272,128]{2,1,0:T(8,128)(2,1)S(1)}, u32[]{:S(2)}, u32[]{:S(2)}) collective-permute-start(bf16[4,272,128]{2,1,0:T(8,128)(2,1)S(1)} %get-tuple-element.89), channel_id=1, source_target_pairs={{0,4},{1,5},{2,6},{3,7},{4,0},{5,1},{6,2},{7,3},{8,12},{9,13},{10,... | collective-permute-start | bytes 835592 | tf_op jit(solution)/shard_map/ppermute | solution.py:743
  274.9 15.8 %collective-permute-start.25 = (bf16[272,128]{1,0:T(8,128)(2,1)S(1)}, bf16[272,128]{1,0:T(8,128)(2,1)S(1)}, u32[]{:S(2)}, u32[]{:S(2)}) collective-permute-start(bf16[272,128]{1,0:T(8,128)(2,1)S(1)} %get-tuple-element.101), channel_id=1, source_target_pairs={{0,8},{1,9},{2,10},{3,11},{4,12},{5,13},{6,14},{7,15},{8,0},{9,1},... | collective-permute-start | bytes 208904 | tf_op jit(solution)/shard_map/ppermute | solution.py:743
  275.0 16.0 %collective-permute-start.27 = (bf16[272,128]{1,0:T(8,128)(2,1)S(1)}, bf16[272,128]{1,0:T(8,128)(2,1)S(1)}, u32[]{:S(2)}, u32[]{:S(2)}) collective-permute-start(bf16[272,128]{1,0:T(8,128)(2,1)S(1)} %get-tuple-element.102), channel_id=1, source_target_pairs={{0,24},{1,25},{2,26},{3,27},{4,28},{5,29},{6,30},{7,31},{8,16},{9,... | collective-permute-start | bytes 208904 | tf_op jit(solution)/shard_map/ppermute | solution.py:743
  285.3 6.0 %collective-permute-start.26 = (bf16[272,128]{1,0:T(8,128)(2,1)S(1)}, bf16[272,128]{1,0:T(8,128)(2,1)S(1)}, u32[]{:S(2)}, u32[]{:S(2)}) collective-permute-start(bf16[272,128]{1,0:T(8,128)(2,1)S(1)} %get-tuple-element.103), channel_id=1, source_target_pairs={{0,16},{1,17},{2,18},{3,19},{4,20},{5,21},{6,22},{7,23},{8,24},{9,... | collective-permute-start | bytes 208904 | tf_op jit(solution)/shard_map/ppermute | solution.py:743
  287.3 31.9 %collective-permute-start.32 = (bf16[272,128]{1,0:T(8,128)(2,1)S(1)}, bf16[272,128]{1,0:T(8,128)(2,1)S(1)}, u32[]{:S(2)}, u32[]{:S(2)}) collective-permute-start(bf16[272,128]{1,0:T(8,128)(2,1)S(1)} %get-tuple-element.97), channel_id=1, source_target_pairs={{0,8},{1,9},{2,10},{3,11},{4,12},{5,13},{6,14},{7,15},{8,0},{9,1},... | collective-permute-start | bytes 208904 | tf_op jit(solution)/shard_map/ppermute | solution.py:743
  287.4 32.6 %collective-permute-start.34 = (bf16[272,128]{1,0:T(8,128)(2,1)S(1)}, bf16[272,128]{1,0:T(8,128)(2,1)S(1)}, u32[]{:S(2)}, u32[]{:S(2)}) collective-permute-start(bf16[272,128]{1,0:T(8,128)(2,1)S(1)} %get-tuple-element.98), channel_id=1, source_target_pairs={{0,24},{1,25},{2,26},{3,27},{4,28},{5,29},{6,30},{7,31},{8,16},{9,... | collective-permute-start | bytes 208904 | tf_op jit(solution)/shard_map/ppermute | solution.py:743
  290.6 15.3 %collective-permute-start.36 = (bf16[4,528,128]{2,1,0:T(8,128)(2,1)S(1)}, bf16[4,528,128]{2,1,0:T(8,128)(2,1)S(1)}, u32[]{:S(2)}, u32[]{:S(2)}) collective-permute-start(bf16[4,528,128]{2,1,0:T(8,128)(2,1)S(1)} %get-tuple-element.84), channel_id=1, source_target_pairs={{0,1},{1,0},{2,3},{3,2},{4,5},{5,4},{6,7},{7,6},{8,9},{9,8},{10,11... | collective-permute-start | bytes 1622024 | tf_op jit(solution)/shard_map/ppermute | solution.py:743
  291.0 22.1 %collective-permute-start.38 = (bf16[4,528,128]{2,1,0:T(8,128)(2,1)S(1)}, bf16[4,528,128]{2,1,0:T(8,128)(2,1)S(1)}, u32[]{:S(2)}, u32[]{:S(2)}) collective-permute-start(bf16[4,528,128]{2,1,0:T(8,128)(2,1)S(1)} %get-tuple-element.85), channel_id=1, source_target_pairs={{0,5},{1,4},{2,7},{3,6},{4,1},{5,0},{6,3},{7,2},{8,13},{9,12},{10,... | collective-permute-start | bytes 1622024 | tf_op jit(solution)/shard_map/ppermute | solution.py:743
  291.3 24.8 %collective-permute-start.37 = (bf16[4,528,128]{2,1,0:T(8,128)(2,1)S(1)}, bf16[4,528,128]{2,1,0:T(8,128)(2,1)S(1)}, u32[]{:S(2)}, u32[]{:S(2)}) collective-permute-start(bf16[4,528,128]{2,1,0:T(8,128)(2,1)S(1)} %get-tuple-element.86), channel_id=1, source_target_pairs={{0,4},{1,5},{2,6},{3,7},{4,0},{5,1},{6,2},{7,3},{8,12},{9,13},{10,... | collective-permute-start | bytes 1622024 | tf_op jit(solution)/shard_map/ppermute | solution.py:743
  305.9 14.1 %collective-permute-start.33 = (bf16[272,128]{1,0:T(8,128)(2,1)S(1)}, bf16[272,128]{1,0:T(8,128)(2,1)S(1)}, u32[]{:S(2)}, u32[]{:S(2)}) collective-permute-start(bf16[272,128]{1,0:T(8,128)(2,1)S(1)} %get-tuple-element.99), channel_id=1, source_target_pairs={{0,16},{1,17},{2,18},{3,19},{4,20},{5,21},{6,22},{7,23},{8,24},{9,... | collective-permute-start | bytes 208904 | tf_op jit(solution)/shard_map/ppermute | solution.py:743
  316.4 5.1 %collective-permute-start.39 = (bf16[528,128]{1,0:T(8,128)(2,1)S(1)}, bf16[528,128]{1,0:T(8,128)(2,1)S(1)}, u32[]{:S(2)}, u32[]{:S(2)}) collective-permute-start(bf16[528,128]{1,0:T(8,128)(2,1)S(1)} %get-tuple-element.93), channel_id=1, source_target_pairs={{0,8},{1,9},{2,10},{3,11},{4,12},{5,13},{6,14},{7,15},{8,0},{9,1},... | collective-permute-start | bytes 405512 | tf_op jit(solution)/shard_map/ppermute | solution.py:743
  316.5 7.7 %collective-permute-start.41 = (bf16[528,128]{1,0:T(8,128)(2,1)S(1)}, bf16[528,128]{1,0:T(8,128)(2,1)S(1)}, u32[]{:S(2)}, u32[]{:S(2)}) collective-permute-start(bf16[528,128]{1,0:T(8,128)(2,1)S(1)} %get-tuple-element.94), channel_id=1, source_target_pairs={{0,24},{1,25},{2,26},{3,27},{4,28},{5,29},{6,30},{7,31},{8,16},{9,... | collective-permute-start | bytes 405512 | tf_op jit(solution)/shard_map/ppermute | solution.py:743
  319.2 9.9 %collective-permute-start.40 = (bf16[528,128]{1,0:T(8,128)(2,1)S(1)}, bf16[528,128]{1,0:T(8,128)(2,1)S(1)}, u32[]{:S(2)}, u32[]{:S(2)}) collective-permute-start(bf16[528,128]{1,0:T(8,128)(2,1)S(1)} %get-tuple-element.95), channel_id=1, source_target_pairs={{0,16},{1,17},{2,18},{3,19},{4,20},{5,21},{6,22},{7,23},{8,24},{9,... | collective-permute-start | bytes 405512 | tf_op jit(solution)/shard_map/ppermute | solution.py:743
  (6 other events, 70.6 us)

commit v2 on v1

--- a/solution.py
+++ b/solution.py
@@ -114,6 +114,11 @@
     block = rows_t[head * HW : (head + 1) * HW, :]
     zero = jnp.zeros_like(block)
     return jnp.concatenate([block, zero] if head % 2 == 0 else [zero, block], 0)
+
+
+def shift_column(shift_ref):
+    row = shift_ref[0] * (LOG2E / math.sqrt(HW))
+    return jnp.broadcast_to(row, (8, row.shape[1])).T[:, :1]
 
 
 def pair_masks(shape, dtype):
@@ -261,7 +266,7 @@
     @pl.when(chunk < nch[item])
     def _():
         scale = tau[item] * (LOG2E / math.sqrt(HW))
-        shift = shift_ref[0] * (LOG2E / math.sqrt(HW))
+        shift = shift_column(shift_ref)
         n1, _ = norm_stats(h_ref[0])
         x1 = n1 * vec1_ref[3:4, :] + vec1_ref[4:5, :]
         q = (dot(x1.astype(bf16), w[:, :D]) + vec[0:1, :]).astype(bf16)
@@ -311,7 +316,7 @@
                 pl.BlockSpec(memory_space=pltpu.SMEM),
                 rowspec,
                 memspec,
-                pl.BlockSpec((1, mem, 1), per_item),
+                pl.BlockSpec((1, 1, mem), per_item),
                 shards, shards,
                 pl.BlockSpec((8, D), whole2, pipeline_mode=pl.Buffered(1)),
             ],
@@ -513,7 +518,7 @@
     def _():
         factor = tau[item] * (1.0 / math.sqrt(HW))
         scale = tau[item] * (LOG2E / math.sqrt(HW))
-        shift = shift_ref[0] * (LOG2E / math.sqrt(HW))
+        shift = shift_column(shift_ref)
         dh2 = dh2_ref[0]
         e2 = dh2.astype(bf16)
         acc[:, 3 * D :] += dot(at_ref[0], e2)
@@ -587,7 +592,7 @@
             in_specs=[
                 pl.BlockSpec(memory_space=pltpu.SMEM),
                 rowspec, rowspec, memspec,
-                pl.BlockSpec((1, mem, 1), per_item),
+                pl.BlockSpec((1, 1, mem), per_item),
                 rowspec, colspec, memspec,
                 pl.BlockSpec((1, D, mem), per_item),
                 memspec, colspec,
@@ -739,8 +744,8 @@
 AXES = ("wide", "narrow")
 
 
-def exchange(rows, offset, count):
-    return lax.ppermute(rows, AXES, [(i, i ^ offset) for i in range(count)])
+def after(value, event):
+    return lax.optimization_barrier((value, event))[0]
 
 
 def offsets(narrow, count):
@@ -756,27 +761,6 @@
     return near + [a ^ core for a in near]
 
 
-def gather_shards(shard, narrow, count):
-    along_z, within, core = offsets(narrow, count)
-    line = jnp.stack([shard] + [exchange(shard, o, count) for o in along_z])
-    near = jnp.concatenate([line] + [exchange(line, o, count) for o in within])
-    return near, exchange(near, core, count)
-
-
-def add_up(parts):
-    return sum(part.astype(f32) for part in parts)
-
-
-def scatter_shards(near, far, narrow, count):
-    along_z, within, core = offsets(narrow, count)
-    depth = 1 + len(along_z)
-    mine = add_up([near, exchange(far, core, count)]).astype(bf16)
-    got = [exchange(mine[(1 + i) * depth : (2 + i) * depth], o, count) for i, o in enumerate(within)]
-    line = add_up([mine[:depth]] + got).astype(bf16)
-    got = [exchange(line[1 + i], o, count) for i, o in enumerate(along_z)]
-    return add_up([line[0]] + got)
-
-
 def to_rows(shard):
     real = shard.shape[0] // LANES
     padded = (real + 15) // 16 * 16
@@ -784,37 +768,82 @@
 
 
 def from_rows(rows, length):
-    return rows[: length // LANES].reshape(length)
+    return rows[0, : length // LANES].reshape(length)
+
+
+def add_up(parts):
+    return sum(part.astype(f32) for part in parts)
 
 
 def body(inputs, memory, tau_scale, delta_shift, horizon, self_params, cross_params, dense_params, cotangent):
     narrow = lax.axis_size("narrow")
     count = lax.axis_size(AXES)
+    along_z, within, core = offsets(narrow, count)
+    depth = 1 + len(along_z)
+
+    def swap(rows, offset):
+        return lax.ppermute(rows, AXES, [(i, i ^ offset) for i in range(count)])
+
+    def line_round(piece):
+        return [piece[None]] + [swap(piece[None], o) for o in along_z]
+
+    def plane_round(line):
+        return [line] + [swap(line, o) for o in within]
+
+    def plane_scatter(mine):
+        return [mine[:depth]] + [swap(mine[depth * i : depth * (i + 1)], o) for i, o in enumerate(within, 1)]
+
+    def line_scatter(line):
+        return [line[:1]] + [swap(line[i : i + 1], o) for i, o in enumerate(along_z, 1)]
+
     x, m, ct = inputs[:, 0], memory[:, 0], cotangent[:, 0]
-    tau, shift, horizon = tau_scale[:, 0], delta_shift[:, 0, :, None], horizon[:, 0]
+    tau, shift, horizon = tau_scale[:, 0], delta_shift, horizon[:, 0]
     order = lax.axis_index(AXES) ^ jnp.array(slot_owners(narrow, count), jnp.int32)
     steps = x.shape[1]
     nch = jnp.minimum((horizon + (LABEL + CH - 1)) // CH, steps // CH).astype(jnp.int32)
     real_a, real_d = self_params.shape[0] // LANES, dense_params.shape[0] // LANES
-    p_self = gather_shards(to_rows(self_params), narrow, count)
-    p_cross = gather_shards(to_rows(cross_params), narrow, count)
-    p_dense = gather_shards(to_rows(dense_params), narrow, count)
-    half, rows = p_self[0].shape[:2]
+    piece_self = to_rows(self_params)
+    piece_rest = jnp.concatenate([to_rows(cross_params), to_rows(dense_params)])
+    cut = piece_self.shape[0]
+
+    line_self = jnp.concatenate(line_round(piece_self))
+    line_rest = line_round(after(piece_rest, line_self))
+    near_self = jnp.concatenate(after(plane_round(line_self), line_rest))
+    p_self = near_self, swap(near_self, core)
+    plane_rest = plane_round(jnp.concatenate(after(line_rest, p_self)))
     q, qt, k, kt, v, at, h1, lse, w1, vec1 = self_forward(nch, order, tau, x, p_self, real_a)
+    plane_rest = after(plane_rest, vec1)
+    near_cross = jnp.concatenate([p[:, :cut] for p in plane_rest])
+    near_dense = jnp.concatenate([p[:, cut:] for p in plane_rest])
+    p_cross = near_cross, swap(near_cross, core)
+    far_dense = swap(after(near_dense, p_cross), core)
     q2, qt2, k2, kt2, v2, at2, h2, lse2, w2, vec2 = cross_forward(nch, order, tau, h1, m, shift, p_cross, vec1, real_a)
-    y, dh2, gn, gf, small2 = dense_both(nch, order, horizon, h2, ct, p_dense, vec2, real_d)
-    g_dense = scatter_shards(gn, gf, narrow, count)
-    dh1, gm, gn, gf, small1 = cross_backward(
-        nch, order, tau, dh2, h1, m, shift, (q2, qt2, k2, kt2, v2, at2, lse2), w2, vec1, small2, half, rows, real_a
+    p_dense = after((near_dense, far_dense), vec2)
+    y, dh2, gn_dense, gf_dense, small2 = dense_both(nch, order, horizon, h2, ct, p_dense, vec2, real_d)
+    other_dense = swap(gf_dense, core)
+    half, rows, _ = near_self.shape
+    dh1, gm, gn_cross, gf_cross, small1 = cross_backward(
+        nch, order, tau, after(dh2, gf_dense), h1, m, shift, (q2, qt2, k2, kt2, v2, at2, lse2), w2, vec1, small2, half, rows, real_a
     )
-    g_cross = scatter_shards(gn, gf, narrow, count)
-    gx, gn, gf = self_backward(nch, order, tau, dh1, x, (q, qt, k, kt, v, at, lse), w1, small1, half, rows, real_a)
-    g_self = scatter_shards(gn, gf, narrow, count)
+    other_cross = swap(gf_cross, core)
+    mine_rest = jnp.concatenate(
+        [add_up([gn_cross, other_cross]).astype(bf16), add_up([gn_dense, after(other_dense, small1)]).astype(bf16)], 1
+    )
+    plane_rest = plane_scatter(mine_rest)
+    gx, gn_self, gf_self = self_backward(
+        nch, order, tau, after(dh1, mine_rest), x, (q, qt, k, kt, v, at, lse), w1, small1, half, rows, real_a
+    )
+    plane_rest, gf_self = after((plane_rest, gf_self), gn_self)
+    other_self = swap(gf_self, core)
+    line_rest = line_scatter(add_up(plane_rest).astype(bf16))
+    plane_self = plane_scatter(add_up([gn_self, other_self]).astype(bf16))
+    line_self = line_scatter(add_up(plane_self).astype(bf16))
+    rest = add_up(after(line_rest, line_self))
     return (
         y[:, None], gx[:, None], gm[:, None],
-        from_rows(g_self, self_params.shape[0]),
-        from_rows(g_cross, cross_params.shape[0]),
-        from_rows(g_dense, dense_params.shape[0]),
+        from_rows(add_up(line_self), self_params.shape[0]),
+        from_rows(rest[:, :cut], cross_params.shape[0]),
+        from_rows(rest[:, cut:], dense_params.shape[0]),
     )
 
 

time: 332 us -> 274 us (0.83)
  waiting for transfers between devices: 86.2 us -> 37.7 us
  starting transfers between devices: 99.5 us -> 64.3 us
  Pallas kernels: 123 us -> 152 us
  local copies, waits for them, and re-layouts: 13.6 us -> 6.36 us
    ppermute x42 -> x30, waiting for transfers between devices: 86.2 us -> 37.7 us  [swap(): return lax.ppermute(rows, AXES, [(i, i ^ offset) for i in range(count)])]
    ppermute x42 -> x30, starting transfers between devices: 99.5 us -> 64.3 us  [swap(): return lax.ppermute(rows, AXES, [(i, i ^ offset) for i in range(count)])]
    pallas_call x1, Pallas kernels: 30.1 us -> 45.9 us  [self_backward(): pl.pallas_call(functools.partial(self_backward_kernel, real=real, chunks=...]
    unnamed x42 -> x26, local copies, waits for them, and re-layouts: 9.79 us -> 3.41 us
    pallas_call x1, Pallas kernels: 33.4 us -> 37.5 us  [dense_both(): pl.pallas_call(functools.partial(dense_kernel, real=real), grid_spec=pltp...]
    pallas_call x1, Pallas kernels: 22.3 us -> 26.1 us  [self_forward(): pl.pallas_call(functools.partial(self_forward_kernel, real=real, chunks=c...]
  transfers between devices with their start and end apart: 42 -> 30, of which waited for: 20 -> 13; matrix products, arithmetic and copies ran while one was open for 5% -> 2% of each run, Pallas kernels for 12% -> 42%
where the time goes in v2:
time: 274 us; the launch traced here: 271 us
  Pallas kernels  152 us (55%)
  starting transfers between devices  64.3 us (23%)
  waiting for transfers between devices  37.7 us (14%)
  other arithmetic  9.39 us (3%)
  local copies, waits for them, and re-layouts  6.36 us (2%)
    ppermute x30, starting transfers between devices, swap(): return lax.ppermute(rows, AXES, [(i, i ^ offset) for i in range(count)])  64.3 us
    pallas_call x1, Pallas kernels, self_backward(): pl.pallas_call(functools.partial(self_backward_kernel, real=real, chunks=...  45.9 us
    ppermute x30, waiting for transfers between devices, swap(): return lax.ppermute(rows, AXES, [(i, i ^ offset) for i in range(count)])  37.7 us
    pallas_call x1, Pallas kernels, dense_both(): pl.pallas_call(functools.partial(dense_kernel, real=real), grid_spec=pltp...  37.5 us
    pallas_call x1, Pallas kernels, self_forward(): pl.pallas_call(functools.partial(self_forward_kernel, real=real, chunks=c...  26.1 us
    pallas_call x1, Pallas kernels, cross_backward(): pl.pallas_call(functools.partial(cross_backward_kernel, real=real), grid_...  22.8 us
    pallas_call x1, Pallas kernels, cross_forward(): pl.pallas_call(functools.partial(cross_forward_kernel, real=real, mem=mem...  19.8 us
  transfers between devices with their start and end apart: 30, of which 13 were waited for; matrix products, arithmetic and copies ran while one was open for 2% of the time, Pallas kernels for 42%

profile of v2, /device:TPU:0, one launch (start us, length us, event | category | flops | bytes accessed | tf_op | source)
XLA Modules:
  0.0 271.1 jit_solution(4616952045004011975)
XLA Ops:
  0.6 0.9 pad_bitcast_fusion
  1.5 5.1 %collective-permute-start.2 = (bf16[1,272,128]{2,1,0:T(8,128)(2,1)S(1)}, bf16[1,272,128]{2,1,0:T(8,128)(2,1)S(1)}, u32[]{:S(2)}, u32[]{:S(2)}) collective-permute-start(bf16[1,272,128]{2,1,0:T(8,128)(2,1)S(1)} %pad_bitcast_fusion), channel_id=1, source_target_pairs={{0,24},{1,25},{2,26},{3,27},{4,28},{5,29},{6,30},{7,31},{8,16},{9,... | collective-permute-start | bytes 208904 | tf_op jit(solution)/shard_map/ppermute | solution.py:785
  6.6 0.6 collective-permute-start
  7.3 1.0 fusion.6
  8.3 1.1 collective-permute-done.2
  9.3 3.2 %collective-permute-done.1 = bf16[1,272,128]{2,1,0:T(8,128)(2,1)S(1)} collective-permute-done((bf16[1,272,128]{2,1,0:T(8,128)(2,1)S(1)}, bf16[1,272,128]{2,1,0:T(8,128)(2,1)S(1)}, u32[]{:S(2)}, u32[]{:S(2)}) %collective-permute-start.1) | collective-permute-done | bytes 69664 | tf_op jit(solution)/shard_map/ppermute | solution.py:785
  12.6 2.8 %collective-permute-start.8 = (bf16[1,800,128]{2,1,0:T(8,128)(2,1)S(1)}, bf16[1,800,128]{2,1,0:T(8,128)(2,1)S(1)}, u32[]{:S(2)}, u32[]{:S(2)}) collective-permute-start(bf16[1,800,128]{2,1,0:T(8,128)(2,1)S(1)} %bitcast.27), channel_id=1, source_target_pairs={{0,24},{1,25},{2,26},{3,27},{4,28},{5,29},{6,30},{7,31},{8,16},{9,... | collective-permute-start | bytes 614408 | tf_op jit(solution)/shard_map/ppermute | solution.py:785
  15.4 2.4 collective-permute-start.5
  17.8 0.5 collective-permute-start.4
  18.3 0.5 collective-permute-start.3
  18.9 3.7 %collective-permute-done.8 = bf16[1,800,128]{2,1,0:T(8,128)(2,1)S(1)} collective-permute-done((bf16[1,800,128]{2,1,0:T(8,128)(2,1)S(1)}, bf16[1,800,128]{2,1,0:T(8,128)(2,1)S(1)}, u32[]{:S(2)}, u32[]{:S(2)}) %collective-permute-start.8) | collective-permute-done | bytes 204832 | tf_op jit(solution)/shard_map/ppermute | solution.py:785
  22.5 7.8 %collective-permute-start.6 = (bf16[1,800,128]{2,1,0:T(8,128)(2,1)S(1)}, bf16[1,800,128]{2,1,0:T(8,128)(2,1)S(1)}, u32[]{:S(2)}, u32[]{:S(2)}) collective-permute-start(bf16[1,800,128]{2,1,0:T(8,128)(2,1)S(1)} %bitcast.29), channel_id=1, source_target_pairs={{0,8},{1,9},{2,10},{3,11},{4,12},{5,13},{6,14},{7,15},{8,0},{9,1},... | collective-permute-start | bytes 614408 | tf_op jit(solution)/shard_map/ppermute | solution.py:785
  30.4 1.7 collective-permute-done.7
  32.0 2.2 collective-permute-done.6
  34.5 0.6 fusion.7.nch
  35.1 2.3 collective-permute-done.9.pf_ref
  37.5 2.6 collective-permute-start.12
  40.1 0.5 collective-permute-start.11
  40.6 0.5 collective-permute-start.10
  41.1 0.5 broadcast_xor_fusion.order
  41.6 26.1 %self_forward.1 = (bf16[2,768,512]{2,1,0:T(8,128)(2,1)}, bf16[2,512,768]{2,1,0:T(8,128)(2,1)}, bf16[2,768,512]{2,1,0:T(8,128)(2,1)}, bf16[2,512,768]{2,1,0:T(8,1...) custom-call(s32[2]{0:T(128)} %fusion.7.nch, ...), custom_call_target="tpu_custom_call" | custom-call | flops 8000000000 | bytes 20000000 | tf_op jit(solution)/shard_map/self_forward/pallas_call | solution.py:205
  67.7 8.6 %collective-permute-done.11 = bf16[4,800,128]{2,1,0:T(8,128)(2,1)S(1)} collective-permute-done((bf16[4,800,128]{2,1,0:T(8,128)(2,1)S(1)}, bf16[4,800,128]{2,1,0:T(8,128)(2,1)S(1)}, u32[]{:S(2)}, u32[]{:S(2)}) %collective-permute-start.11) | collective-permute-done | bytes 819232 | tf_op jit(solution)/shard_map/ppermute | solution.py:785
  76.5 0.7 copy-done.4
  77.6 1.0 copy-done.5
  78.7 1.0 slice-done
  79.9 0.3 collective-permute-done.13.pf_ref
  80.3 1.3 copy-done.7
  81.6 19.8 %cross_forward.1 = (bf16[2,768,512]{2,1,0:T(8,128)(2,1)}, bf16[2,512,768]{2,1,0:T(8,128)(2,1)}, bf16[2,96,512]{2,1,0:T(8,128)(2,1)}, bf16[2,512,96]{2,1,0:T(8,12...) custom-call(s32[2]{0:T(128)} %fusion.7.nch, ...), custom_call_target="tpu_custom_call" | custom-call | flops 4000000000 | bytes 20000000 | tf_op jit(solution)/shard_map/cross_forward/pallas_call | solution.py:310
  101.4 37.5 %dense_both.1 = (bf16[2,768,512]{2,1,0:T(8,128)(2,1)}, f32[2,768,512]{2,1,0:T(8,128)}, bf16[16,528,128]{2,1,0:T(8,128)(2,1)}, bf16[16,528,128]{2,1,0:T(8,128)(2,1)}, f32[8,512]{1,0:T(8,128)}) custom-call(s32[2]{0:T(128)} %fusion.7.nch, s32[32]{0:T(128)} %broadcast_xor_fusion.order, s32[2]{0:T(128)} %bitcast.39, f32[2,768,512]{2,1,0:T(8,128)} %get-tuple-element.82.h_ref, ...), custom_call_target="tpu_custom_call" | custom-call | flops 20000000000 | bytes 30000000 | tf_op jit(solution)/shard_map/dense_both/pallas_call | solution.py:443
  138.9 22.8 %cross_backward.1 = (f32[2,768,512]{2,1,0:T(8,128)}, f32[2,96,512]{2,1,0:T(8,128)}, bf16[16,272,128]{2,1,0:T(8,128)(2,1)}, bf16[16,272,128]{2,1,0:T(8,128)(2,1)}, f32[8,512]{1,0:T(8,128)}) custom-call(s32[2]{0:T(128)} %fusion.7.nch, s32[32]{0:T(128)} %broadcast_xor_fusion.order, f32[2]{0:T(128)} %bitcast.42, f32[2,768,512]{2,1,0:T(8,128)} %get-tuple-element.90.dh2_ref, ...), custom_call_target="tpu_custom_call" | custom-call | flops 8000000000 | bytes 20000000 | tf_op jit(solution)/shard_map/cross_backward/pallas_call | solution.py:587
  161.8 3.0 %collective-permute-done.15 = bf16[16,272,128]{2,1,0:T(8,128)(2,1)S(1)} collective-permute-done((bf16[16,272,128]{2,1,0:T(8,128)(2,1)}, bf16[16,272,128]{2,1,0:T(8,128)(2,1)S(1)}, u32[]{:S(2)}, u32[]{:S(2)}) %collective-permute-start.15) | collective-permute-done | bytes 1114144 | tf_op jit(solution)/shard_map/ppermute | solution.py:785
  164.7 1.7 add_convert_fusion.2
  166.7 0.6 add_convert_fusion
  167.7 3.4 %collective-permute-start.18 = (bf16[4,800,128]{2,1,0:T(8,128)(2,1)S(1)}, bf16[4,800,128]{2,1,0:T(8,128)(2,1)}, u32[]{:S(2)}, u32[]{:S(2)}) collective-permute-start(bf16[4,800,128]{2,1,0:T(8,128)(2,1)S(1)} %get-tuple-element.136), channel_id=1, source_target_pairs={{0,4},{1,5},{2,6},{3,7},{4,0},{5,1},{6,2},{7,3},{8,12},{9,13},{10,... | collective-permute-start | bytes 2457608 | tf_op jit(solution)/shard_map/ppermute | solution.py:785
  171.1 45.9 %self_backward.1 = (f32[2,768,512]{2,1,0:T(8,128)}, bf16[16,272,128]{2,1,0:T(8,128)(2,1)}, bf16[16,272,128]{2,1,0:T(8,128)(2,1)}) custom-call(s32[2]{0:T(128)} %fusion.7.nch, s32[32]{0:T(128)} %broadcast_xor_fusion.order, f32[2]{0:T(128)} %bitcast.43, f32[2,768,512]{2,1,0:T(8,128)} %get-tuple-element.106.dh1_ref, bf16[2,768,512]{2,1,0:T(8,128)(2,1)} %bitcast.36, ...), custom_call_target="tpu_custom_call" | custom-call | flops 15000000512 | bytes 20000000 | tf_op jit(solution)/shard_map/self_backward/pallas_call | solution.py:712
  217.1 3.0 %collective-permute-done.20 = bf16[16,272,128]{2,1,0:T(8,128)(2,1)S(1)} collective-permute-done((bf16[16,272,128]{2,1,0:T(8,128)(2,1)}, bf16[16,272,128]{2,1,0:T(8,128)(2,1)S(1)}, u32[]{:S(2)}, u32[]{:S(2)}) %collective-permute-start.20) | collective-permute-done | bytes 1114144 | tf_op jit(solution)/shard_map/ppermute | solution.py:785
  220.1 1.5 add_convert_fusion.1
  221.8 3.4 %collective-permute-start.22 = (bf16[4,272,128]{2,1,0:T(8,128)(2,1)S(1)}, bf16[4,272,128]{2,1,0:T(8,128)(2,1)S(1)}, u32[]{:S(2)}, u32[]{:S(2)}) collective-permute-start(bf16[4,272,128]{2,1,0:T(8,128)(2,1)S(1)} %get-tuple-element.140), channel_id=1, source_target_pairs={{0,4},{1,5},{2,6},{3,7},{4,0},{5,1},{6,2},{7,3},{8,12},{9,13},{10,... | collective-permute-start | bytes 835592 | tf_op jit(solution)/shard_map/ppermute | solution.py:785
  225.2 1.8 add_convert_fusion.3
  227.1 18.3 %collective-permute-start.29 = (bf16[1,800,128]{2,1,0:T(8,128)(2,1)S(1)}, bf16[1,800,128]{2,1,0:T(8,128)(2,1)S(1)}, u32[]{:S(2)}, u32[]{:S(2)}) collective-permute-start(bf16[1,800,128]{2,1,0:T(8,128)(2,1)S(1)} %get-tuple-element.141), channel_id=1, source_target_pairs={{0,24},{1,25},{2,26},{3,27},{4,28},{5,29},{6,30},{7,31},{8,16},{9,... | collective-permute-start | bytes 614408 | tf_op jit(solution)/shard_map/ppermute | solution.py:785
  245.4 1.5 collective-permute-start.28
  246.8 2.6 collective-permute-start.27
  249.6 8.2 %collective-permute-start.26 = (bf16[1,272,128]{2,1,0:T(8,128)(2,1)S(1)}, bf16[1,272,128]{2,1,0:T(8,128)(2,1)S(1)}, u32[]{:S(2)}, u32[]{:S(2)}) collective-permute-start(bf16[1,272,128]{2,1,0:T(8,128)(2,1)S(1)} %get-tuple-element.146), channel_id=1, source_target_pairs={{0,24},{1,25},{2,26},{3,27},{4,28},{5,29},{6,30},{7,31},{8,16},{9,... | collective-permute-start | bytes 208904 | tf_op jit(solution)/shard_map/ppermute | solution.py:785
  257.8 3.0 %collective-permute-start.24 = (bf16[1,272,128]{2,1,0:T(8,128)(2,1)S(1)}, bf16[1,272,128]{2,1,0:T(8,128)(2,1)S(1)}, u32[]{:S(2)}, u32[]{:S(2)}) collective-permute-start(bf16[1,272,128]{2,1,0:T(8,128)(2,1)S(1)} %get-tuple-element.148), channel_id=1, source_target_pairs={{0,8},{1,9},{2,10},{3,11},{4,12},{5,13},{6,14},{7,15},{8,0},{9,1},... | collective-permute-start | bytes 208904 | tf_op jit(solution)/shard_map/ppermute | solution.py:785
  260.8 5.7 %collective-permute-done.28 = bf16[1,800,128]{2,1,0:T(8,128)(2,1)S(1)} collective-permute-done((bf16[1,800,128]{2,1,0:T(8,128)(2,1)S(1)}, bf16[1,800,128]{2,1,0:T(8,128)(2,1)S(1)}, u32[]{:S(2)}, u32[]{:S(2)}) %collective-permute-start.28) | collective-permute-done | bytes 204832 | tf_op jit(solution)/shard_map/ppermute | solution.py:785
  266.5 2.9 %collective-permute-done.25 = bf16[1,272,128]{2,1,0:T(8,128)(2,1)S(1)} collective-permute-done((bf16[1,272,128]{2,1,0:T(8,128)(2,1)S(1)}, bf16[1,272,128]{2,1,0:T(8,128)(2,1)S(1)}, u32[]{:S(2)}, u32[]{:S(2)}) %collective-permute-start.25) | collective-permute-done | bytes 69664 | tf_op jit(solution)/shard_map/ppermute | solution.py:785
  269.5 0.7 slice_bitcast_fusion
  270.2 0.7 slice_bitcast_fusion.1
  (73 shorter events, 2.7 us)
Async XLA Ops:
  1.5 33.0 %copy-start.8 = (s32[2,1]{0,1:T(1,128)S(1)}, s32[2,1]{0,1:T(1,128)}, u32[]{:S(2)}) copy-start(s32[2,1]{0,1:T(1,128)} %param.14) | copy-start | bytes 28
  1.5 7.8 %collective-permute-start.2 = (bf16[1,272,128]{2,1,0:T(8,128)(2,1)S(1)}, bf16[1,272,128]{2,1,0:T(8,128)(2,1)S(1)}, u32[]{:S(2)}, u32[]{:S(2)}) collective-permute-start(bf16[1,272,128]{2,1,0:T(8,128)(2,1)S(1)} %pad_bitcast_fusion), channel_id=1, source_target_pairs={{0,24},{1,25},{2,26},{3,27},{4,28},{5,29},{6,30},{7,31},{8,16},{9,... | collective-permute-start | bytes 208904 | tf_op jit(solution)/shard_map/ppermute | solution.py:785
  6.6 5.9 %collective-permute-start.1 = (bf16[1,272,128]{2,1,0:T(8,128)(2,1)S(1)}, bf16[1,272,128]{2,1,0:T(8,128)(2,1)S(1)}, u32[]{:S(2)}, u32[]{:S(2)}) collective-permute-start(bf16[1,272,128]{2,1,0:T(8,128)(2,1)S(1)} %pad_bitcast_fusion), channel_id=1, source_target_pairs={{0,16},{1,17},{2,18},{3,19},{4,20},{5,21},{6,22},{7,23},{8,24},{9,... | collective-permute-start | bytes 208904 | tf_op jit(solution)/shard_map/ppermute | solution.py:785
  6.6 5.9 %collective-permute-start = (bf16[1,272,128]{2,1,0:T(8,128)(2,1)S(1)}, bf16[1,272,128]{2,1,0:T(8,128)(2,1)S(1)}, u32[]{:S(2)}, u32[]{:S(2)}) collective-permute-start(bf16[1,272,128]{2,1,0:T(8,128)(2,1)S(1)} %pad_bitcast_fusion), channel_id=1, source_target_pairs={{0,8},{1,9},{2,10},{3,11},{4,12},{5,13},{6,14},{7,15},{8,0},{9,1},... | collective-permute-start | bytes 208904 | tf_op jit(solution)/shard_map/ppermute | solution.py:785
  12.6 9.9 %collective-permute-start.8 = (bf16[1,800,128]{2,1,0:T(8,128)(2,1)S(1)}, bf16[1,800,128]{2,1,0:T(8,128)(2,1)S(1)}, u32[]{:S(2)}, u32[]{:S(2)}) collective-permute-start(bf16[1,800,128]{2,1,0:T(8,128)(2,1)S(1)} %bitcast.27), channel_id=1, source_target_pairs={{0,24},{1,25},{2,26},{3,27},{4,28},{5,29},{6,30},{7,31},{8,16},{9,... | collective-permute-start | bytes 614408 | tf_op jit(solution)/shard_map/ppermute | solution.py:785
  15.4 18.8 %collective-permute-start.5 = (bf16[4,272,128]{2,1,0:T(8,128)(2,1)S(1)}, bf16[4,272,128]{2,1,0:T(8,128)(2,1)S(1)}, u32[]{:S(2)}, u32[]{:S(2)}) collective-permute-start(bf16[4,272,128]{2,1,0:T(8,128)(2,1)S(1)} %pad_maximum_fusion.3), channel_id=1, source_target_pairs={{0,5},{1,4},{2,7},{3,6},{4,1},{5,0},{6,3},{7,2},{8,13},{9,12},{10,... | collective-permute-start | bytes 835592 | tf_op jit(solution)/shard_map/ppermute | solution.py:785
  17.8 16.4 %collective-permute-start.4 = (bf16[4,272,128]{2,1,0:T(8,128)(2,1)S(1)}, bf16[4,272,128]{2,1,0:T(8,128)(2,1)S(1)}, u32[]{:S(2)}, u32[]{:S(2)}) collective-permute-start(bf16[4,272,128]{2,1,0:T(8,128)(2,1)S(1)} %pad_maximum_fusion.3), channel_id=1, source_target_pairs={{0,4},{1,5},{2,6},{3,7},{4,0},{5,1},{6,2},{7,3},{8,12},{9,13},{10,... | collective-permute-start | bytes 835592 | tf_op jit(solution)/shard_map/ppermute | solution.py:785
  18.3 15.9 %collective-permute-start.3 = (bf16[4,272,128]{2,1,0:T(8,128)(2,1)S(1)}, bf16[4,272,128]{2,1,0:T(8,128)(2,1)S(1)}, u32[]{:S(2)}, u32[]{:S(2)}) collective-permute-start(bf16[4,272,128]{2,1,0:T(8,128)(2,1)S(1)} %pad_maximum_fusion.3), channel_id=1, source_target_pairs={{0,1},{1,0},{2,3},{3,2},{4,5},{5,4},{6,7},{7,6},{8,9},{9,8},{10,11... | collective-permute-start | bytes 835592 | tf_op jit(solution)/shard_map/ppermute | solution.py:785
  18.9 13.2 %collective-permute-start.7 = (bf16[1,800,128]{2,1,0:T(8,128)(2,1)S(1)}, bf16[1,800,128]{2,1,0:T(8,128)(2,1)S(1)}, u32[]{:S(2)}, u32[]{:S(2)}) collective-permute-start(bf16[1,800,128]{2,1,0:T(8,128)(2,1)S(1)} %bitcast.28), channel_id=1, source_target_pairs={{0,16},{1,17},{2,18},{3,19},{4,20},{5,21},{6,22},{7,23},{8,24},{9,... | collective-permute-start | bytes 614408 | tf_op jit(solution)/shard_map/ppermute | solution.py:785
  22.5 11.7 %collective-permute-start.6 = (bf16[1,800,128]{2,1,0:T(8,128)(2,1)S(1)}, bf16[1,800,128]{2,1,0:T(8,128)(2,1)S(1)}, u32[]{:S(2)}, u32[]{:S(2)}) collective-permute-start(bf16[1,800,128]{2,1,0:T(8,128)(2,1)S(1)} %bitcast.29), channel_id=1, source_target_pairs={{0,8},{1,9},{2,10},{3,11},{4,12},{5,13},{6,14},{7,15},{8,0},{9,1},... | collective-permute-start | bytes 614408 | tf_op jit(solution)/shard_map/ppermute | solution.py:785
  34.3 6.8 %copy-start.9 = (s32[32]{0:T(128)S(1)}, s32[32]{0:T(128)}, u32[]{:S(2)}) copy-start(s32[32]{0:T(128)} %constant.35.clone) | copy-start | bytes 388
  34.4 3.1 %copy-start.6 = (bf16[16,272,128]{2,1,0:T(8,128)(2,1)}, bf16[16,272,128]{2,1,0:T(8,128)(2,1)S(1)}, u32[]{:S(2)}) copy-start(bf16[16,272,128]{2,1,0:T(8,128)(2,1)S(1)} %constant_dynamic-update-slice_fusion.pn_ref) | copy-start | bytes 3342340
  34.4 3.0 %collective-permute-start.9 = (bf16[16,272,128]{2,1,0:T(8,128)(2,1)S(1)}, bf16[16,272,128]{2,1,0:T(8,128)(2,1)}, u32[]{:S(2)}, u32[]{:S(2)}) collective-permute-start(bf16[16,272,128]{2,1,0:T(8,128)(2,1)S(1)} %constant_dynamic-update-slice_fusion.pn_ref), channel_id=1, source_target_pairs={{0,2},{1,3},{2,0},{3,1},{4,6},{5,7},{6,4},{7,5},{8,10},{9,11},{10,... | collective-permute-start | bytes 3342344 | tf_op jit(solution)/shard_map/ppermute | solution.py:785
  37.5 30.2 %collective-permute-start.12 = (bf16[4,800,128]{2,1,0:T(8,128)(2,1)S(1)}, bf16[4,800,128]{2,1,0:T(8,128)(2,1)S(1)}, u32[]{:S(2)}, u32[]{:S(2)}) collective-permute-start(bf16[4,800,128]{2,1,0:T(8,128)(2,1)S(1)} %constant_dynamic-update-slice_fusion.4), channel_id=1, source_target_pairs={{0,5},{1,4},{2,7},{3,6},{4,1},{5,0},{6,3},{7,2},{8,13},{9,12},{10,... | collective-permute-start | bytes 2457608 | tf_op jit(solution)/shard_map/ppermute | solution.py:785
  40.1 36.2 %collective-permute-start.11 = (bf16[4,800,128]{2,1,0:T(8,128)(2,1)S(1)}, bf16[4,800,128]{2,1,0:T(8,128)(2,1)S(1)}, u32[]{:S(2)}, u32[]{:S(2)}) collective-permute-start(bf16[4,800,128]{2,1,0:T(8,128)(2,1)S(1)} %constant_dynamic-update-slice_fusion.4), channel_id=1, source_target_pairs={{0,4},{1,5},{2,6},{3,7},{4,0},{5,1},{6,2},{7,3},{8,12},{9,13},{10,... | collective-permute-start | bytes 2457608 | tf_op jit(solution)/shard_map/ppermute | solution.py:785
  40.6 35.9 %collective-permute-start.10 = (bf16[4,800,128]{2,1,0:T(8,128)(2,1)S(1)}, bf16[4,800,128]{2,1,0:T(8,128)(2,1)S(1)}, u32[]{:S(2)}, u32[]{:S(2)}) collective-permute-start(bf16[4,800,128]{2,1,0:T(8,128)(2,1)S(1)} %constant_dynamic-update-slice_fusion.4), channel_id=1, source_target_pairs={{0,1},{1,0},{2,3},{3,2},{4,5},{5,4},{6,7},{7,6},{8,9},{9,8},{10,11... | collective-permute-start | bytes 2457608 | tf_op jit(solution)/shard_map/ppermute | solution.py:785
  76.3 0.9 copy-start.4
  76.5 1.1 copy-start.1
  77.3 1.3 copy-start.5
  77.4 1.2 copy-start.3
  77.4 2.8 %collective-permute-start.13 = (bf16[16,272,128]{2,1,0:T(8,128)(2,1)S(1)}, bf16[16,272,128]{2,1,0:T(8,128)(2,1)S(1)}, u32[]{:S(2)}, u32[]{:S(2)}) collective-permute-start(bf16[16,272,128]{2,1,0:T(8,128)(2,1)S(1)} %pad_maximum_fusion.2.pn_ref), channel_id=1, source_target_pairs={{0,2},{1,3},{2,0},{3,1},{4,6},{5,7},{6,4},{7,5},{8,10},{9,11},{10,... | collective-permute-start | bytes 3342344 | tf_op jit(solution)/shard_map/ppermute | solution.py:785
  78.6 1.0 slice-start
  79.9 21.5 %copy-start.2 = (bf16[16,528,128]{2,1,0:T(8,128)(2,1)}, bf16[16,528,128]{2,1,0:T(8,128)(2,1)S(1)}, u32[]{:S(2)}) copy-start(bf16[16,528,128]{2,1,0:T(8,128)(2,1)S(1)} %pad_maximum_fusion.1.pn_ref) | copy-start | bytes 6488068
  80.2 1.3 copy-start.7
  81.5 19.9 %collective-permute-start.14 = (bf16[16,528,128]{2,1,0:T(8,128)(2,1)S(1)}, bf16[16,528,128]{2,1,0:T(8,128)(2,1)}, u32[]{:S(2)}, u32[]{:S(2)}) collective-permute-start(bf16[16,528,128]{2,1,0:T(8,128)(2,1)S(1)} %pad_maximum_fusion.1.pn_ref), channel_id=1, source_target_pairs={{0,2},{1,3},{2,0},{3,1},{4,6},{5,7},{6,4},{7,5},{8,10},{9,11},{10,... | collective-permute-start | bytes 6488072 | tf_op jit(solution)/shard_map/ppermute | solution.py:785
  138.9 27.5 %collective-permute-start.16 = (bf16[16,528,128]{2,1,0:T(8,128)(2,1)}, bf16[16,528,128]{2,1,0:T(8,128)(2,1)S(1)}, u32[]{:S(2)}, u32[]{:S(2)}) collective-permute-start(bf16[16,528,128]{2,1,0:T(8,128)(2,1)} %get-tuple-element.89), channel_id=1, source_target_pairs={{0,2},{1,3},{2,0},{3,1},{4,6},{5,7},{6,4},{7,5},{8,10},{9,11},{10,... | collective-permute-start | bytes 6488072 | tf_op jit(solution)/shard_map/ppermute | solution.py:785
  161.7 3.0 %collective-permute-start.15 = (bf16[16,272,128]{2,1,0:T(8,128)(2,1)}, bf16[16,272,128]{2,1,0:T(8,128)(2,1)S(1)}, u32[]{:S(2)}, u32[]{:S(2)}) collective-permute-start(bf16[16,272,128]{2,1,0:T(8,128)(2,1)} %get-tuple-element.102), channel_id=1, source_target_pairs={{0,2},{1,3},{2,0},{3,1},{4,6},{5,7},{6,4},{7,5},{8,10},{9,11},{10,... | collective-permute-start | bytes 3342344 | tf_op jit(solution)/shard_map/ppermute | solution.py:785
  164.7 1.9 copy-start
  167.5 49.5 %collective-permute-start.19 = (bf16[4,800,128]{2,1,0:T(8,128)(2,1)S(1)}, bf16[4,800,128]{2,1,0:T(8,128)(2,1)S(1)}, u32[]{:S(2)}, u32[]{:S(2)}) collective-permute-start(bf16[4,800,128]{2,1,0:T(8,128)(2,1)S(1)} %get-tuple-element.134), channel_id=1, source_target_pairs={{0,5},{1,4},{2,7},{3,6},{4,1},{5,0},{6,3},{7,2},{8,13},{9,12},{10,... | collective-permute-start | bytes 2457608 | tf_op jit(solution)/shard_map/ppermute | solution.py:785
  167.6 49.4 %collective-permute-start.17 = (bf16[4,800,128]{2,1,0:T(8,128)(2,1)S(1)}, bf16[4,800,128]{2,1,0:T(8,128)(2,1)}, u32[]{:S(2)}, u32[]{:S(2)}) collective-permute-start(bf16[4,800,128]{2,1,0:T(8,128)(2,1)S(1)} %get-tuple-element.135), channel_id=1, source_target_pairs={{0,1},{1,0},{2,3},{3,2},{4,5},{5,4},{6,7},{7,6},{8,9},{9,8},{10,11... | collective-permute-start | bytes 2457608 | tf_op jit(solution)/shard_map/ppermute | solution.py:785
  167.7 49.3 %collective-permute-start.18 = (bf16[4,800,128]{2,1,0:T(8,128)(2,1)S(1)}, bf16[4,800,128]{2,1,0:T(8,128)(2,1)}, u32[]{:S(2)}, u32[]{:S(2)}) collective-permute-start(bf16[4,800,128]{2,1,0:T(8,128)(2,1)S(1)} %get-tuple-element.136), channel_id=1, source_target_pairs={{0,4},{1,5},{2,6},{3,7},{4,0},{5,1},{6,2},{7,3},{8,12},{9,13},{10,... | collective-permute-start | bytes 2457608 | tf_op jit(solution)/shard_map/ppermute | solution.py:785
  217.0 3.0 %collective-permute-start.20 = (bf16[16,272,128]{2,1,0:T(8,128)(2,1)}, bf16[16,272,128]{2,1,0:T(8,128)(2,1)S(1)}, u32[]{:S(2)}, u32[]{:S(2)}) collective-permute-start(bf16[16,272,128]{2,1,0:T(8,128)(2,1)} %get-tuple-element.119), channel_id=1, source_target_pairs={{0,2},{1,3},{2,0},{3,1},{4,6},{5,7},{6,4},{7,5},{8,10},{9,11},{10,... | collective-permute-start | bytes 3342344 | tf_op jit(solution)/shard_map/ppermute | solution.py:785
  221.7 25.2 %collective-permute-start.21 = (bf16[4,272,128]{2,1,0:T(8,128)(2,1)S(1)}, bf16[4,272,128]{2,1,0:T(8,128)(2,1)S(1)}, u32[]{:S(2)}, u32[]{:S(2)}) collective-permute-start(bf16[4,272,128]{2,1,0:T(8,128)(2,1)S(1)} %get-tuple-element.138), channel_id=1, source_target_pairs={{0,1},{1,0},{2,3},{3,2},{4,5},{5,4},{6,7},{7,6},{8,9},{9,8},{10,11... | collective-permute-start | bytes 835592 | tf_op jit(solution)/shard_map/ppermute | solution.py:785
  221.7 27.7 %collective-permute-start.23 = (bf16[4,272,128]{2,1,0:T(8,128)(2,1)S(1)}, bf16[4,272,128]{2,1,0:T(8,128)(2,1)S(1)}, u32[]{:S(2)}, u32[]{:S(2)}) collective-permute-start(bf16[4,272,128]{2,1,0:T(8,128)(2,1)S(1)} %get-tuple-element.139), channel_id=1, source_target_pairs={{0,5},{1,4},{2,7},{3,6},{4,1},{5,0},{6,3},{7,2},{8,13},{9,12},{10,... | collective-permute-start | bytes 835592 | tf_op jit(solution)/shard_map/ppermute | solution.py:785
  221.8 27.6 %collective-permute-start.22 = (bf16[4,272,128]{2,1,0:T(8,128)(2,1)S(1)}, bf16[4,272,128]{2,1,0:T(8,128)(2,1)S(1)}, u32[]{:S(2)}, u32[]{:S(2)}) collective-permute-start(bf16[4,272,128]{2,1,0:T(8,128)(2,1)S(1)} %get-tuple-element.140), channel_id=1, source_target_pairs={{0,4},{1,5},{2,6},{3,7},{4,0},{5,1},{6,2},{7,3},{8,12},{9,13},{10,... | collective-permute-start | bytes 835592 | tf_op jit(solution)/shard_map/ppermute | solution.py:785
  227.1 30.7 %collective-permute-start.29 = (bf16[1,800,128]{2,1,0:T(8,128)(2,1)S(1)}, bf16[1,800,128]{2,1,0:T(8,128)(2,1)S(1)}, u32[]{:S(2)}, u32[]{:S(2)}) collective-permute-start(bf16[1,800,128]{2,1,0:T(8,128)(2,1)S(1)} %get-tuple-element.141), channel_id=1, source_target_pairs={{0,24},{1,25},{2,26},{3,27},{4,28},{5,29},{6,30},{7,31},{8,16},{9,... | collective-permute-start | bytes 614408 | tf_op jit(solution)/shard_map/ppermute | solution.py:785
  245.4 21.1 %collective-permute-start.28 = (bf16[1,800,128]{2,1,0:T(8,128)(2,1)S(1)}, bf16[1,800,128]{2,1,0:T(8,128)(2,1)S(1)}, u32[]{:S(2)}, u32[]{:S(2)}) collective-permute-start(bf16[1,800,128]{2,1,0:T(8,128)(2,1)S(1)} %get-tuple-element.142), channel_id=1, source_target_pairs={{0,16},{1,17},{2,18},{3,19},{4,20},{5,21},{6,22},{7,23},{8,24},{9,... | collective-permute-start | bytes 614408 | tf_op jit(solution)/shard_map/ppermute | solution.py:785
  246.8 19.6 %collective-permute-start.27 = (bf16[1,800,128]{2,1,0:T(8,128)(2,1)S(1)}, bf16[1,800,128]{2,1,0:T(8,128)(2,1)S(1)}, u32[]{:S(2)}, u32[]{:S(2)}) collective-permute-start(bf16[1,800,128]{2,1,0:T(8,128)(2,1)S(1)} %get-tuple-element.143), channel_id=1, source_target_pairs={{0,8},{1,9},{2,10},{3,11},{4,12},{5,13},{6,14},{7,15},{8,0},{9,1},... | collective-permute-start | bytes 614408 | tf_op jit(solution)/shard_map/ppermute | solution.py:785
  249.6 16.9 %collective-permute-start.26 = (bf16[1,272,128]{2,1,0:T(8,128)(2,1)S(1)}, bf16[1,272,128]{2,1,0:T(8,128)(2,1)S(1)}, u32[]{:S(2)}, u32[]{:S(2)}) collective-permute-start(bf16[1,272,128]{2,1,0:T(8,128)(2,1)S(1)} %get-tuple-element.146), channel_id=1, source_target_pairs={{0,24},{1,25},{2,26},{3,27},{4,28},{5,29},{6,30},{7,31},{8,16},{9,... | collective-permute-start | bytes 208904 | tf_op jit(solution)/shard_map/ppermute | solution.py:785
  257.8 11.6 %collective-permute-start.25 = (bf16[1,272,128]{2,1,0:T(8,128)(2,1)S(1)}, bf16[1,272,128]{2,1,0:T(8,128)(2,1)S(1)}, u32[]{:S(2)}, u32[]{:S(2)}) collective-permute-start(bf16[1,272,128]{2,1,0:T(8,128)(2,1)S(1)} %get-tuple-element.147), channel_id=1, source_target_pairs={{0,16},{1,17},{2,18},{3,19},{4,20},{5,21},{6,22},{7,23},{8,24},{9,... | collective-permute-start | bytes 208904 | tf_op jit(solution)/shard_map/ppermute | solution.py:785
  257.8 11.6 %collective-permute-start.24 = (bf16[1,272,128]{2,1,0:T(8,128)(2,1)S(1)}, bf16[1,272,128]{2,1,0:T(8,128)(2,1)S(1)}, u32[]{:S(2)}, u32[]{:S(2)}) collective-permute-start(bf16[1,272,128]{2,1,0:T(8,128)(2,1)S(1)} %get-tuple-element.148), channel_id=1, source_target_pairs={{0,8},{1,9},{2,10},{3,11},{4,12},{5,13},{6,14},{7,15},{8,0},{9,1},... | collective-permute-start | bytes 208904 | tf_op jit(solution)/shard_map/ppermute | solution.py:785
